TPU v7x, 32 devices: a whole 2x2x4 slice. The times are simulated.
32 devices in a mesh: date: 4 (over y, x), az: 8 (over z, core).
Axes of the slice: x: 2, y: 2, z: 4, core: 2. Of those that a mesh axis runs over, the one named last changes fastest.
Arguments:
- epoch_image_tensor: bfloat16 [16, 2, 2560, 1280], P('date', None, 'az'), may hold values from -5 to 5
- along_track_shifts: int32 [16, 40, 20], P('date', 'az'), may hold values from -32 to 32, as said below
- cross_track_shifts: int32 [16, 40, 20], P('date', 'az'), may hold values from -32 to 32, as said below
- epoch_present_table: int32 [16, 40], P('date', 'az'), may hold values 0 or 1
Outputs:
- tile_similarity: float32 [16, 40, 20], P('date', 'az')
- smoothed_ifgs: float32 [16, 2, 512, 64], P('date', None, 'az')
Inputs may be any that keep to these rules, and one draw needn't show every extreme that they name: `along_track_shifts`: date 0 has all offsets zero. `cross_track_shifts`: date 0 has all offsets zero.
All inputs are finite; a program needn't handle non-finite values. Where the computation divides by a largest or mean magnitude, that divisor is 1e-20 or more. No bound on the sum of `epoch_present_table` on one device may be relied on, other than what follows from the above.
Results may differ from a plain program's by a relative error of at most 0.0003.
Values may be sent and summed in bfloat16 or wider, within the bound.
A program may use at most 192 MiB of HBM per device.

v0:
```python
import jax
import jax.numpy as jnp
import numpy as np
from jax import lax
from jax.experimental import pallas as pl
from jax.experimental.pallas import tpu as pltpu
from jax.sharding import PartitionSpec as P

WIN = 64
MARGIN = 32
LOOK_AZ = 5
LOOK_RG = 20
PATCH = 32
LANES = 128
PIECE = 16
AHEAD = 8
LAG = 5
OPENING = 4

VAR_EPS = 1e-05
RMS_EPS = 1e-06
TINY = 1e-37

F32 = jnp.float32
BF16 = jnp.bfloat16


def tables(lines, samples):
    turns = np.outer(np.arange(PATCH), np.arange(PATCH)) % PATCH
    angles = turns * (2.0 * np.pi / PATCH)
    two = np.eye(2)
    cosine = np.kron(two, np.cos(angles))
    sine = np.kron(two, np.sin(angles))
    rows_fwd = np.block([[cosine, sine], [-sine, cosine]])
    cols_fwd = np.block([[cosine, -sine], [sine, cosine]])
    dft = np.stack([rows_fwd, cols_fwd]).astype(np.float32)
    near = np.abs(np.arange(PATCH)[:, None] - np.arange(PATCH)[None, :])
    circular = np.minimum(near, PATCH - near) <= 1
    four = np.eye(LANES // PATCH)
    half = np.kron(np.eye(2), np.ones((WIN, WIN)))
    blocks = np.stack(
        [half, np.kron(four, circular), np.kron(four, np.ones((PATCH, PATCH)))]
    ).astype(np.float32)
    az_pool = (
        np.arange(lines // LOOK_AZ)[:, None] == np.arange(lines)[None, :] // LOOK_AZ
    ).astype(np.float32)
    rg_pool = (
        np.arange(samples)[:, None] // LOOK_RG == np.arange(samples // LOOK_RG)[None, :]
    ).astype(np.float32)
    rg_pool = np.concatenate([rg_pool, rg_pool], axis=0)
    return (
        jnp.asarray(dft),
        jnp.asarray(blocks, BF16),
        jnp.asarray(az_pool, BF16),
        jnp.asarray(rg_pool, BF16),
    )


def dot(a, b):
    return jnp.dot(a, b, preferred_element_type=F32)


def dot_high(a, b):
    a_high, a_low = split(a)
    b_high, b_low = split(b)
    return dot(a_high, b_high) + (dot(a_high, b_low) + dot(a_low, b_high))


def split(x):
    high = x.astype(BF16)
    return high, (x - high.astype(F32)).astype(BF16)


def dot_right(x, ones):
    high, low = split(x)
    return dot(high, ones) + dot(low, ones)


def dot_left(ones, x):
    high, low = split(x)
    return dot(ones, high) + dot(ones, low)


def root(x):
    return x * lax.rsqrt(jnp.maximum(x, TINY))


def resample(p, d, sizes, at_ref, ct_ref, pr_ref, wide, shifted, devs, stats):
    dates, lines, strips = sizes
    lane = lax.broadcasted_iota(jnp.int32, (WIN, LANES), 1)
    first = lane < WIN
    near_low = lane < LANES - MARGIN
    near_high = lane < MARGIN
    present = pr_ref[d, p]
    here = pl.ds(pl.multiple_of(p * WIN, WIN), WIN)
    for m in range(strips):
        rows = []
        turns = []
        for q in (2 * m, 2 * m + 1):
            start = jnp.where(
                present != 0, p * WIN + MARGIN + at_ref[p, d, q], lines + 2 * MARGIN
            )
            rows.append(pl.ds(start, WIN))
            turns.append((LANES - ct_ref[p, d, q]) % LANES)
        part = []
        for c in range(2):
            even = wide[d, c, m, rows[0], :]
            below = wide[d, c, m - 1, rows[0], :] if m > 0 else jnp.zeros_like(even)
            odd = wide[d, c, m, rows[1], :]
            above = wide[d, c, m + 1, rows[1], :] if m + 1 < strips else jnp.zeros_like(odd)
            even = pltpu.roll(jnp.where(near_low, even, below), turns[0], 1)
            odd = pltpu.roll(jnp.where(near_high, above, odd), turns[1], 1)
            part.append(jnp.where(first, even, odd))
            shifted[d, c, m, here, :] = part[c]
        amp = root(part[0] * part[0] + part[1] * part[1]).reshape(WIN // 8, 8, LANES)
        mean = jnp.sum(amp, axis=0) * (8.0 / WIN)
        dev = amp - mean[None]
        devs[d, m, here, :] = dev.reshape(WIN, LANES)
        stats[p, 0, m, d] = mean
        stats[p, 1, m, d] = jnp.sum(dev * dev, axis=0)


def window_row(p, sizes, ref_chunk, blk_ref, rgp_ref, shifted, devs, band, prod, pooled, stats, sims, follow):
    dates, lines, strips = sizes
    for m in range(strips):
        cols = slice(m * LANES, (m + 1) * LANES)
        real = ref_chunk(0, cols)
        imag = ref_chunk(1, cols)
        band[0, m] = real
        band[1, m] = imag
        amp = root(real * real + imag * imag).reshape(WIN // 8, 8, LANES)
        mean = jnp.sum(amp, axis=0) * (8.0 / WIN)
        dev = amp - mean[None]
        band[2, m] = dev.reshape(WIN, LANES)
        stats[p, 0, m, dates] = mean
        stats[p, 1, m, dates] = jnp.sum(dev * dev, axis=0)

    def one_date(d, carry):
        follow(d)
        here = pl.ds(pl.multiple_of(p * WIN, WIN), WIN)
        for m in range(strips):
            sr = shifted[d, 0, m, here, :]
            si = shifted[d, 1, m, here, :]
            joint = devs[d, m, here, :] * band[2, m]
            stats[p, 2, m, d] = jnp.sum(joint.reshape(WIN // 8, 8, LANES), axis=0)
            rr = band[0, m]
            ri = band[1, m]
            for c, value in enumerate((rr * sr + ri * si, ri * sr - rr * si)):
                high, low = split(value)
                prod[d, c, :, m * LANES : (m + 1) * LANES] = high
                prod[d, c, :, (strips + m) * LANES : (strips + m + 1) * LANES] = low
        return carry

    lax.fori_loop(0, dates, one_date, 0)
    width = 2 * strips * LANES
    sums = dot(prod[...].reshape(dates * 2 * WIN, width), rgp_ref[...])
    pooled[:, :, pl.ds(pl.multiple_of(p * WIN, WIN), WIN), :] = sums.reshape(dates, 2, WIN, -1)

    half = blk_ref[0]

    def total(x):
        flat = x.reshape(-1, LANES)
        return jnp.sum(dot_right(flat, half).reshape(-1, 8, LANES), axis=1, keepdims=True)

    count = 8.0 * WIN
    means = stats[p, 0].reshape(strips * (dates + 1), 8, LANES)
    away = means - total(means) * (1.0 / count)
    spread = stats[p, 1].reshape(strips * (dates + 1), 8, LANES)
    var = total(spread + (WIN / 8.0) * (away * away)) * (1.0 / (WIN * WIN))
    away = away.reshape(strips, dates + 1, 8, LANES)
    var = var.reshape(strips, dates + 1, 1, LANES)
    joint = stats[p, 2][:, :dates] + (WIN / 8.0) * (away[:, :dates] * away[:, dates:])
    cov = total(joint).reshape(strips, dates, 1, LANES) * (1.0 / (WIN * WIN))
    corr = cov / jnp.sqrt((var[:, dates:] + VAR_EPS) * (var[:, :dates] + VAR_EPS))
    lane = lax.broadcasted_iota(jnp.int32, (dates, 1, LANES), 2)
    found = jnp.zeros((dates, 1, LANES), F32)
    for m in range(strips):
        here = corr[m]
        other = pltpu.roll(here.reshape(dates, LANES), WIN, 1).reshape(dates, 1, LANES)
        left = jnp.where(lane < WIN, here, other)
        right = jnp.where(lane < WIN, other, here)
        found = jnp.where(lane == 2 * m, left, jnp.where(lane == 2 * m + 1, right, found))
    sims[p] = found


def goldstein(dates, out_ref, dft_ref, blk_ref, azp_ref, pooled):
    az_pool = azp_ref[...]
    looks_az = az_pool.shape[0]
    rows_fwd = dft_ref[0]
    cols_fwd = dft_ref[1]

    def rows_to_cols(x):
        return jnp.concatenate([x[:looks_az], x[looks_az:]], axis=1)

    turned = []
    for d in range(dates):
        z = jnp.concatenate([dot_left(az_pool, pooled[d, c]) for c in range(2)], axis=0)
        turned.append(rows_to_cols(dot_high(rows_fwd, z)))
    spectrum = dot_high(jnp.concatenate(turned, axis=0), cols_fwd)
    squares = spectrum * spectrum
    magnitude = root(squares + pltpu.roll(squares, WIN, 1))
    smooth = dot_right(magnitude, blk_ref[1]).reshape(-1, PATCH, LANES)
    smooth = (
        smooth
        + jnp.concatenate([smooth[:, 1:], smooth[:, :1]], axis=1)
        + jnp.concatenate([smooth[:, -1:], smooth[:, :-1]], axis=1)
    ).reshape(spectrum.shape)
    weighted = spectrum * root(smooth * (1.0 / 9.0))
    turned = []
    for d in range(dates):
        w = weighted[d * looks_az : (d + 1) * looks_az]
        w = jnp.concatenate([w[:, :WIN], w[:, WIN:]], axis=0)
        turned.append(rows_to_cols(dot_high(cols_fwd, w)))
    back = dot_high(jnp.concatenate(turned, axis=0), rows_fwd)
    squares = back * back
    power = dot_right(squares + pltpu.roll(squares, WIN, 1), blk_ref[2]).reshape(-1, PATCH, LANES)
    power = jnp.sum(power, axis=1, keepdims=True) * (1.0 / (PATCH * PATCH))
    scaled = back.reshape(-1, PATCH, LANES) * lax.rsqrt(power + RMS_EPS)
    scaled = scaled.reshape(back.shape)
    for d in range(dates):
        rows = scaled[d * looks_az : (d + 1) * looks_az]
        out_ref[d, 0] = rows[:, :WIN]
        out_ref[d, 1] = rows[:, WIN:]


def ring_device(position, count):
    half = count // 2
    return jnp.where(position < half, 2 * position, 2 * (count - 1 - position) + 1)


def kernel(
    at_ref, ct_ref, pr_ref, img_ref, blk_ref, rgp_ref,
    sim_ref, pooled,
    image, halo, ref, wide, shifted, devs, band, prod, stats, sims,
    image_sem, root_sem, halo_send, halo_recv, ref_send, ref_recv,
):
    dates, _, lines, samples = img_ref.shape
    strips = samples // LANES
    rows = lines // WIN
    pieces = ref_send.shape[1]
    height = lines // pieces
    each = WIN // height
    count = lax.axis_size("date")
    az_count = lax.axis_size("az")
    az = lax.axis_index("az")
    mine = lax.axis_index("date")
    position = jnp.where(mine % 2 == 0, mine // 2, count - 1 - mine // 2)
    after = ring_device((position + 1) % count, count)
    before = ring_device((position + count - 1) % count, count)
    hops = (position, (count - position) % count)
    targets = (after, before)
    mesh_ids = pl.DeviceIdType.MESH

    def load(i):
        d = i // 2
        c = i % 2
        return pltpu.make_async_copy(img_ref.at[d, c], image.at[d, c], image_sem.at[i])

    for i in range(2 * dates):
        load(i).start()
    own = pltpu.make_async_copy(img_ref.at[0], ref, root_sem)

    @pl.when(mine == 0)
    def _():
        own.start()

    barrier = pltpu.get_barrier_semaphore()
    for target in targets:
        pl.semaphore_signal(barrier, inc=1, device_id={"date": target}, device_id_type=mesh_ids)

    @pl.when(az > 0)
    def _():
        pl.semaphore_signal(barrier, inc=1, device_id={"az": az - 1}, device_id_type=mesh_ids)

    @pl.when(az < az_count - 1)
    def _():
        pl.semaphore_signal(barrier, inc=1, device_id={"az": az + 1}, device_id_type=mesh_ids)

    peers = 2 + jnp.where(az > 0, 1, 0) + jnp.where(az < az_count - 1, 1, 0)
    pl.semaphore_wait(barrier, peers)

    def row_of(s):
        return jnp.where(s < rows - 2, s + 1, jnp.where(s == rows - 2, 0, rows - 1))

    def piece_rows(j):
        return pl.ds(pl.multiple_of(row_of(j // each) * WIN + (j % each) * height, height), height)

    def relay(c, j, first):
        at = piece_rows(j)
        return pltpu.make_async_remote_copy(
            src_ref=img_ref.at[0, c, at] if first else ref.at[c, at],
            dst_ref=ref.at[c, at],
            send_sem=ref_send.at[c, j],
            recv_sem=ref_recv.at[c, j],
            device_id={"date": targets[c]},
            device_id_type=mesh_ids,
        )

    def launch(j):
        for c in range(2):
            relay(c, j, True).start()

    def slot(t):
        for c in range(2):
            j = t - (hops[c] - 1) * LAG
            here = (hops[c] > 0) & (j >= 0) & (j < pieces)

            @pl.when(here)
            def _():
                relay(c, j, False).wait_recv()

            @pl.when(here & (hops[c] < count - 1))
            def _():
                relay(c, j, False).start()

        @pl.when((mine == 0) & (t + AHEAD < pieces))
        def _():
            launch(t + AHEAD)

    @pl.when(mine == 0)
    def _():
        for j in range(AHEAD):
            launch(j)

    def edge(k):
        start = 0 if k else lines - MARGIN
        return pltpu.make_async_remote_copy(
            src_ref=img_ref.at[:, :, pl.ds(start, MARGIN)],
            dst_ref=halo.at[k],
            send_sem=halo_send.at[k],
            recv_sem=halo_recv.at[k],
            device_id={"az": az - 1 if k else az + 1},
            device_id_type=mesh_ids,
        )

    sends = (az < az_count - 1, az > 0)
    takes = (az > 0, az < az_count - 1)
    for k in range(2):
        @pl.when(sends[k])
        def _():
            edge(k).start()

    def widen(i, carry):
        d = i // 2
        c = i % 2
        load(i).wait()
        for m in range(strips):
            cols = slice(m * LANES, (m + 1) * LANES)
            wide[d, c, m, MARGIN : MARGIN + lines, :] = image[d, c, :, cols].astype(F32)
            wide[d, c, m, 2 * MARGIN + lines : 2 * MARGIN + lines + WIN, :] = jnp.zeros((WIN, LANES), F32)

        @pl.when(i >= 2 * dates - opening)
        def _():
            slot(i - (2 * dates - opening))

        return carry

    early = each + (count - 2) * LAG
    opening = min(OPENING, 2 * dates)
    lax.fori_loop(0, 2 * dates, widen, 0)

    def fringe(k):
        first = MARGIN + lines if k else 0

        @pl.when(takes[k])
        def _():
            edge(k).wait_recv()

            def convert(i, carry):
                d = i // 2
                c = i % 2
                for m in range(strips):
                    cols = slice(m * LANES, (m + 1) * LANES)
                    wide[d, c, m, first : first + MARGIN, :] = halo[k, d, c, :, cols].astype(F32)
                return carry

            lax.fori_loop(0, 2 * dates, convert, 0)

        @pl.when(jnp.logical_not(takes[k]))
        def _():
            def clear(i, carry):
                for m in range(strips):
                    wide[i // 2, i % 2, m, first : first + MARGIN, :] = jnp.zeros((MARGIN, LANES), F32)
                return carry

            lax.fori_loop(0, 2 * dates, clear, 0)

    share = -(-(early - opening) // (dates * rows))
    pace = max(1, dates * rows // max(1, early - opening))

    def shift(i, carry):
        s = i // dates

        @pl.when((i % pace) == 0)
        def _():
            for e in range(share):
                t = opening + (i // pace) * share + e

                @pl.when(t < early)
                def _():
                    slot(t)

        @pl.when(i == (rows - 2) * dates)
        def _():
            for k in range(2):
                fringe(k)

        resample(row_of(s), i % dates, (dates, lines, strips), at_ref, ct_ref, pr_ref, wide, shifted, devs, stats)
        return carry

    lax.fori_loop(0, dates * rows, shift, 0)

    @pl.when(mine == 0)
    def _():
        own.wait()

    def row(s, carry):
        p = row_of(s)

        def ref_chunk(c, cols):
            return ref[c, pl.ds(pl.multiple_of(p * WIN, WIN), WIN), cols].astype(F32)

        def follow(d):
            share = -(-each // dates)
            for e in range(share):
                k = d * share + e

                @pl.when((s < rows - 1) & (k < each))
                def _():
                    slot(early + s * each + k)

        window_row(
            p, (dates, lines, strips), ref_chunk, blk_ref, rgp_ref,
            shifted, devs, band, prod, pooled, stats, sims, follow,
        )
        return carry

    lax.fori_loop(0, rows, row, 0)
    for p in range(rows):
        sim_ref[p] = sims[p].reshape(dates, LANES)[:, : sim_ref.shape[2]]

    for c in range(2):
        @pl.when(hops[c] < count - 1)
        def _():
            def drain(j, carry):
                relay(c, j, False).wait_send()
                return carry

            lax.fori_loop(0, pieces, drain, 0)

    for k in range(2):
        @pl.when(sends[k])
        def _():
            edge(k).wait_send()


def finish(found_ref, pooled_ref, dft_ref, blk_ref, azp_ref, sim_ref, out_ref):
    sim_ref[...] = found_ref[...]
    goldstein(out_ref.shape[0], out_ref, dft_ref, blk_ref, azp_ref, pooled_ref)


def on_device(image, along, cross, present):
    dates, _, lines, samples = image.shape
    strips = samples // LANES
    rows = lines // WIN
    pieces = lines // PIECE
    smem = pl.BlockSpec(memory_space=pltpu.SMEM)
    vmem = pl.BlockSpec(memory_space=pltpu.VMEM)
    dma = pltpu.SemaphoreType.DMA
    dft, blocks, az_pool, rg_pool = tables(lines, samples)
    similarity, pooled = pl.pallas_call(
        kernel,
        out_shape=(
            jax.ShapeDtypeStruct((rows, dates, samples // WIN), F32),
            jax.ShapeDtypeStruct((dates, 2, lines, samples // LOOK_RG), F32),
        ),
        in_specs=[smem] * 3 + [pl.BlockSpec(memory_space=pl.ANY)] + [vmem] * 2,
        out_specs=(vmem, vmem),
        scratch_shapes=[
            pltpu.VMEM((dates, 2, lines, samples), BF16),
            pltpu.VMEM((2, dates, 2, MARGIN, samples), BF16),
            pltpu.VMEM((2, lines, samples), BF16),
            pltpu.VMEM((dates, 2, strips, lines + 2 * MARGIN + WIN, LANES), F32),
            pltpu.VMEM((dates, 2, strips, lines, LANES), F32),
            pltpu.VMEM((dates, strips, lines, LANES), F32),
            pltpu.VMEM((3, strips, WIN, LANES), F32),
            pltpu.VMEM((dates, 2, WIN, 2 * samples), BF16),
            pltpu.VMEM((rows, 3, strips, dates + 1, 8, LANES), F32),
            pltpu.VMEM((rows, dates, 1, LANES), F32),
            dma((2 * dates,)),
            dma(()),
            dma((2,)),
            dma((2,)),
            dma((2, pieces)),
            dma((2, pieces)),
        ],
        compiler_params=pltpu.CompilerParams(
            vmem_limit_bytes=62 * 1024 * 1024, collective_id=0, has_side_effects=True
        ),
    )(
        along.transpose(1, 0, 2), cross.transpose(1, 0, 2), present, image, blocks, rg_pool
    )
    similarity, filtered = pl.pallas_call(
        finish,
        out_shape=(
            jax.ShapeDtypeStruct(similarity.shape, F32),
            jax.ShapeDtypeStruct((dates, 2, lines // LOOK_AZ, samples // LOOK_RG), F32),
        ),
        in_specs=[vmem] * 5,
        out_specs=(vmem, vmem),
    )(similarity, pooled, dft, blocks, az_pool)
    return similarity.transpose(1, 0, 2), filtered


def solution(mesh):
    placed = (
        P("date", None, "az", None),
        P("date", "az", None),
        P("date", "az", None),
        P("date", "az"),
    )
    return jax.shard_map(
        on_device,
        mesh=mesh,
        in_specs=placed,
        out_specs=(P("date", "az", None), P("date", None, "az", None)),
        check_vma=False,
    )
```

profile of v0, /device:TPU:10, one launch (start us, length us, event | category | flops | bytes accessed | tf_op | source)
XLA Modules:
  0.0 41.3 jit_solution(12063138825304572666)
XLA Ops:
  0.6 36.2 %shard_map.95 = (f32[5,4,20]{2,1,0:T(4,128)}, f32[4,2,320,64]{3,2,1,0:T(8,128)}) custom-call(s32[5,4,20]{2,1,0:T(4,128)} %bitcast.3, s32[5,4,20]{2,1,0:T(4,128)} %bitcast.4, s32[4,5]{1,0:T(4,128)} %pr_ref.1, bf16[4,2,320,1280]{3,2,1,0:T(8,128)(2,1)} %img_ref.1, bf16[3,128,128]{2,1,0:T(8,128)(2,1)} %constant.9.clone.blk_ref, ...), custom_call_target="tpu_custom_call" | custom-call | tf_op jit(solution)/shard_map/pallas_call | solution.py:471
  36.8 4.4 %shard_map.96 = (f32[5,4,20]{2,1,0:T(4,128)}, f32[4,2,64,64]{3,2,1,0:T(8,128)}) custom-call(f32[5,4,20]{2,1,0:T(4,128)} %get-tuple-element.6.found_ref, f32[4,2,320,64]{3,2,1,0:T(8,128)} %get-tuple-element.7.pooled_ref, f32[2,128,128]{2,1,0:T(8,128)} %constant.8.clone.dft_ref, bf16[3,128,128]{2,1,0:T(8,128)(2,1)} %constant.9.clone.blk_ref, ...), custom_call_target="tpu_custom_call" | custom-call | tf_op jit(solution)/shard_map/pallas_call | solution.py:503
where the time goes:
time: 41.4 us; the launch traced here: 41.3 us
  Pallas kernels  40.6 us (98%)
  between operations  0.64 us (2%)
    pallas_call x1, Pallas kernels, on_device(): pl.pallas_call(kernel, out_shape=(jax.ShapeDtypeStruct((rows, dates, samp...  36.2 us
    pallas_call x1, Pallas kernels, on_device(): pl.pallas_call(finish, out_shape=(jax.ShapeDtypeStruct(similarity.shape,...  4.44 us

commit v1 on v0

v1 whole, which is shorter than its diff:
```python
import jax
import jax.numpy as jnp
import numpy as np
from jax import lax
from jax.experimental import pallas as pl
from jax.experimental.pallas import tpu as pltpu
from jax.sharding import PartitionSpec as P

WIN = 64
MARGIN = 32
LOOK_AZ = 5
LOOK_RG = 20
PATCH = 32
LANES = 128
PIECE = 16
LAG = 3
PACE = 3

VAR_EPS = 1e-05
RMS_EPS = 1e-06
TINY = 1e-37

F32 = jnp.float32
BF16 = jnp.bfloat16


def tables(samples):
    turns = np.outer(np.arange(PATCH), np.arange(PATCH)) % PATCH
    angles = turns * (2.0 * np.pi / PATCH)
    two = np.eye(2)
    cosine = np.kron(two, np.cos(angles))
    sine = np.kron(two, np.sin(angles))
    rows_fwd = np.block([[cosine, sine], [-sine, cosine]])
    cols_fwd = np.block([[cosine, -sine], [sine, cosine]])
    dft = np.stack([rows_fwd, cols_fwd]).astype(np.float32)
    near = np.abs(np.arange(PATCH)[:, None] - np.arange(PATCH)[None, :])
    circular = np.minimum(near, PATCH - near) <= 1
    four = np.eye(LANES // PATCH)
    half = np.kron(np.eye(2), np.ones((WIN, WIN)))
    blocks = np.stack(
        [half, np.kron(four, circular), np.kron(four, np.ones((PATCH, PATCH)))]
    ).astype(np.float32)
    rg_pool = (
        np.arange(samples)[:, None] // LOOK_RG == np.arange(samples // LOOK_RG)[None, :]
    ).astype(np.float32)
    return (
        jnp.asarray(dft),
        jnp.asarray(blocks, BF16),
        jnp.asarray(rg_pool, BF16),
    )


def dot(a, b):
    return jnp.dot(a, b, preferred_element_type=F32)


def dot_high(a, b):
    a_high, a_low = split(a)
    b_high, b_low = split(b)
    return dot(a_high, b_high) + (dot(a_high, b_low) + dot(a_low, b_high))


def split(x):
    high = x.astype(BF16)
    return high, (x - high.astype(F32)).astype(BF16)


def dot_right(x, ones):
    high, low = split(x)
    return dot(high, ones) + dot(low, ones)


def root(x):
    return x * lax.rsqrt(jnp.maximum(x, TINY))


def resample(p, d, sizes, at_ref, ct_ref, pr_ref, wide, shifted, devs, stats):
    dates, lines, strips = sizes
    lane = lax.broadcasted_iota(jnp.int32, (WIN, LANES), 1)
    first = lane < WIN
    near_low = lane < LANES - MARGIN
    near_high = lane < MARGIN
    present = pr_ref[d, p]
    here = pl.ds(pl.multiple_of(p * WIN, WIN), WIN)
    for m in range(strips):
        rows = []
        turns = []
        for q in (2 * m, 2 * m + 1):
            start = jnp.where(
                present != 0, p * WIN + MARGIN + at_ref[p, d, q], lines + 2 * MARGIN
            )
            rows.append(pl.ds(start, WIN))
            turns.append((LANES - ct_ref[p, d, q]) & (LANES - 1))
        part = []
        for c in range(2):
            even = wide[d, c, m, rows[0], :]
            below = wide[d, c, m - 1, rows[0], :] if m > 0 else jnp.zeros_like(even)
            odd = wide[d, c, m, rows[1], :]
            above = wide[d, c, m + 1, rows[1], :] if m + 1 < strips else jnp.zeros_like(odd)
            even = pltpu.roll(jnp.where(near_low, even, below).astype(BF16), turns[0], 1)
            odd = pltpu.roll(jnp.where(near_high, above, odd).astype(BF16), turns[1], 1)
            part.append(jnp.where(first, even, odd).astype(F32))
            shifted[d, c, m, here, :] = part[c]
        amp = root(part[0] * part[0] + part[1] * part[1]).reshape(WIN // 8, 8, LANES)
        mean = jnp.sum(amp, axis=0) * (8.0 / WIN)
        dev = amp - mean[None]
        devs[d, m, here, :] = dev.reshape(WIN, LANES)
        stats[p, 0, m, d] = mean
        stats[p, 1, m, d] = jnp.sum(dev * dev, axis=0)


def prepare(p, sizes, ref, ref32, devs, stats):
    dates, lines, strips = sizes
    here = pl.ds(pl.multiple_of(p * WIN, WIN), WIN)
    for m in range(strips):
        cols = slice(m * LANES, (m + 1) * LANES)
        real = ref[0, here, cols].astype(F32)
        imag = ref[1, here, cols].astype(F32)
        ref32[0, m, here, :] = real
        ref32[1, m, here, :] = imag
        amp = root(real * real + imag * imag).reshape(WIN // 8, 8, LANES)
        mean = jnp.sum(amp, axis=0) * (8.0 / WIN)
        dev = amp - mean[None]
        stats[p, 0, m, dates] = mean
        stats[p, 1, m, dates] = jnp.sum(dev * dev, axis=0)
        for d in range(dates):
            joint = devs[d, m, here, :].reshape(WIN // 8, 8, LANES) * dev
            stats[p, 2, m, d] = jnp.sum(joint, axis=0)


def similarity(p, sizes, blk_ref, stats, sim_ref):
    dates, lines, strips = sizes
    half = blk_ref[0]

    def total(x):
        flat = x.reshape(-1, LANES)
        return jnp.sum(dot_right(flat, half).reshape(-1, 8, LANES), axis=1, keepdims=True)

    count = 8.0 * WIN
    means = stats[p, 0].reshape(strips * (dates + 1), 8, LANES)
    away = means - total(means) * (1.0 / count)
    spread = stats[p, 1].reshape(strips * (dates + 1), 8, LANES)
    var = total(spread + (WIN / 8.0) * (away * away)) * (1.0 / (WIN * WIN))
    away = away.reshape(strips, dates + 1, 8, LANES)
    var = var.reshape(strips, dates + 1, 1, LANES)
    joint = stats[p, 2][:, :dates] + (WIN / 8.0) * (away[:, :dates] * away[:, dates:])
    cov = total(joint).reshape(strips, dates, 1, LANES) * (1.0 / (WIN * WIN))
    corr = cov / jnp.sqrt((var[:, dates:] + VAR_EPS) * (var[:, :dates] + VAR_EPS))
    lane = lax.broadcasted_iota(jnp.int32, (dates, 1, LANES), 2)
    found = jnp.zeros((dates, 1, LANES), F32)
    for m in range(strips):
        here = corr[m]
        other = pltpu.roll(here.reshape(dates, LANES), WIN, 1).reshape(dates, 1, LANES)
        left = jnp.where(lane < WIN, here, other)
        right = jnp.where(lane < WIN, other, here)
        found = jnp.where(lane == 2 * m, left, jnp.where(lane == 2 * m + 1, right, found))
    sim_ref[p] = found.reshape(dates, LANES)[:, : sim_ref.shape[2]]


def interferogram(g, sizes, rgp_ref, ref32, shifted, prod, pooled):
    dates, lines, strips = sizes
    rows = [pl.ds(g * (8 * LOOK_AZ) + k, 8, stride=LOOK_AZ) for k in range(LOOK_AZ)]
    for m in range(strips):
        cols = slice(m * LANES, (m + 1) * LANES)
        rr = [ref32[0, m, at, :] for at in rows]
        ri = [ref32[1, m, at, :] for at in rows]
        for d in range(dates):
            real = imag = 0.0
            for k, at in enumerate(rows):
                sr = shifted[d, 0, m, at, :]
                si = shifted[d, 1, m, at, :]
                real = real + (rr[k] * sr + ri[k] * si)
                imag = imag + (ri[k] * sr - rr[k] * si)
            high, low = split(jnp.concatenate([real, imag], axis=0))
            prod[0, d, :, cols] = high
            prod[1, d, :, cols] = low
    sums = dot(prod[...].reshape(2 * dates * 16, strips * LANES), rgp_ref[...])
    sums = (sums[: dates * 16] + sums[dates * 16 :]).reshape(dates, 2, 8, -1)
    groups = PATCH // 8
    at = pl.ds(pl.multiple_of((g % groups) * 8, 8), 8)
    for d in range(dates):
        for c in range(2):
            pooled[g // groups, d // 2, c, d % 2, at, :] = sums[d, c]


def goldstein(h, dates, out_ref, dft_ref, blk_ref, pooled):
    rows_fwd = dft_ref[0]
    cols_fwd = dft_ref[1]
    pairs = dates // 2

    def rows_to_cols(x):
        return jnp.concatenate([x[:WIN], x[WIN:]], axis=1)

    turned = []
    for e in range(pairs):
        z = pooled[h, e].reshape(2 * WIN, -1)
        turned.append(rows_to_cols(dot_high(rows_fwd, z)))
    spectrum = dot_high(jnp.concatenate(turned, axis=0), cols_fwd)
    squares = spectrum * spectrum
    magnitude = root(squares + pltpu.roll(squares, WIN, 1))
    smooth = dot_right(magnitude, blk_ref[1]).reshape(-1, PATCH, LANES)
    smooth = (
        smooth
        + jnp.concatenate([smooth[:, 1:], smooth[:, :1]], axis=1)
        + jnp.concatenate([smooth[:, -1:], smooth[:, :-1]], axis=1)
    ).reshape(spectrum.shape)
    weighted = spectrum * root(smooth * (1.0 / 9.0))
    turned = []
    for e in range(pairs):
        w = weighted[e * WIN : (e + 1) * WIN]
        w = jnp.concatenate([w[:, :WIN], w[:, WIN:]], axis=0)
        turned.append(rows_to_cols(dot_high(cols_fwd, w)))
    back = dot_high(jnp.concatenate(turned, axis=0), rows_fwd)
    squares = back * back
    power = dot_right(squares + pltpu.roll(squares, WIN, 1), blk_ref[2]).reshape(-1, PATCH, LANES)
    power = jnp.sum(power, axis=1, keepdims=True) * (1.0 / (PATCH * PATCH))
    scaled = back.reshape(-1, PATCH, LANES) * lax.rsqrt(power + RMS_EPS)
    at = pl.ds(pl.multiple_of(h * PATCH, PATCH), PATCH)
    for d in range(dates):
        out_ref[d, 0, at, :] = scaled[d][:, :WIN]
        out_ref[d, 1, at, :] = scaled[d][:, WIN:]


def ring_device(position, count):
    half = count // 2
    return jnp.where(position < half, 2 * position, 2 * (count - 1 - position) + 1)


def kernel(
    at_ref, ct_ref, pr_ref, img_ref, dft_ref, blk_ref, rgp_ref,
    sim_ref, out_ref,
    image, halo, ref, wide, shifted, devs, ref32, prod, pooled, stats,
    image_sem, root_sem, halo_send, halo_recv, ref_send, ref_recv,
):
    dates, _, lines, samples = img_ref.shape
    strips = samples // LANES
    rows = lines // WIN
    pieces = ref_send.shape[1]
    height = lines // pieces
    each = WIN // height
    groups = lines // (8 * LOOK_AZ)
    halves = lines // (LOOK_AZ * PATCH)
    sizes = (dates, lines, strips)
    count = lax.axis_size("date")
    az_count = lax.axis_size("az")
    az = lax.axis_index("az")
    mine = lax.axis_index("date")
    position = jnp.where(mine % 2 == 0, mine // 2, count - 1 - mine // 2)
    after = ring_device((position + 1) % count, count)
    before = ring_device((position + count - 1) % count, count)
    hops = (position, (count - position) % count)
    targets = (after, before)
    mesh_ids = pl.DeviceIdType.MESH

    def load(i):
        d = i // 2
        c = i % 2
        return pltpu.make_async_copy(img_ref.at[d, c], image.at[d, c], image_sem.at[i])

    for i in range(2 * dates):
        load(i).start()
    own = pltpu.make_async_copy(img_ref.at[0], ref, root_sem)

    @pl.when(mine == 0)
    def _():
        own.start()

    barrier = pltpu.get_barrier_semaphore()
    for target in targets:
        pl.semaphore_signal(barrier, inc=1, device_id={"date": target}, device_id_type=mesh_ids)

    @pl.when(az > 0)
    def _():
        pl.semaphore_signal(barrier, inc=1, device_id={"az": az - 1}, device_id_type=mesh_ids)

    @pl.when(az < az_count - 1)
    def _():
        pl.semaphore_signal(barrier, inc=1, device_id={"az": az + 1}, device_id_type=mesh_ids)

    peers = 2 + jnp.where(az > 0, 1, 0) + jnp.where(az < az_count - 1, 1, 0)
    pl.semaphore_wait(barrier, peers)

    def relay(c, j, first):
        at = pl.ds(pl.multiple_of(j * height, height), height)
        return pltpu.make_async_remote_copy(
            src_ref=img_ref.at[0, c, at] if first else ref.at[c, at],
            dst_ref=ref.at[c, at],
            send_sem=ref_send.at[c, j],
            recv_sem=ref_recv.at[c, j],
            device_id={"date": targets[c]},
            device_id_type=mesh_ids,
        )

    @pl.when(mine == 0)
    def _():
        def launch(j, carry):
            for c in range(2):
                relay(c, j, True).start()
            return carry

        lax.fori_loop(0, pieces, launch, 0)

    def slot(t):
        for c in range(2):
            j = t - (hops[c] - 1) * LAG

            @pl.when((hops[c] > 0) & (hops[c] < count - 1) & (j >= 0) & (j < pieces))
            def _():
                relay(c, j, False).wait_recv()
                relay(c, j, False).start()

    def edge(k):
        start = 0 if k else lines - MARGIN
        return pltpu.make_async_remote_copy(
            src_ref=img_ref.at[:, :, pl.ds(start, MARGIN)],
            dst_ref=halo.at[k],
            send_sem=halo_send.at[k],
            recv_sem=halo_recv.at[k],
            device_id={"az": az - 1 if k else az + 1},
            device_id_type=mesh_ids,
        )

    sends = (az < az_count - 1, az > 0)
    takes = (az > 0, az < az_count - 1)
    for k in range(2):
        @pl.when(sends[k])
        def _():
            edge(k).start()

    def widen(i, carry):
        d = i // 2
        c = i % 2
        load(i).wait()
        for m in range(strips):
            cols = slice(m * LANES, (m + 1) * LANES)
            wide[d, c, m, MARGIN : MARGIN + lines, :] = image[d, c, :, cols].astype(F32)
            wide[d, c, m, 2 * MARGIN + lines : 2 * MARGIN + lines + WIN, :] = jnp.zeros((WIN, LANES), F32)
        return carry

    lax.fori_loop(0, 2 * dates, widen, 0)
    slot(0)

    def fringe(k):
        first = MARGIN + lines if k else 0

        @pl.when(takes[k])
        def _():
            edge(k).wait_recv()

            def convert(i, carry):
                d = i // 2
                c = i % 2
                for m in range(strips):
                    cols = slice(m * LANES, (m + 1) * LANES)
                    wide[d, c, m, first : first + MARGIN, :] = halo[k, d, c, :, cols].astype(F32)
                return carry

            lax.fori_loop(0, 2 * dates, convert, 0)

        @pl.when(jnp.logical_not(takes[k]))
        def _():
            def clear(i, carry):
                for m in range(strips):
                    wide[i // 2, i % 2, m, first : first + MARGIN, :] = jnp.zeros((MARGIN, LANES), F32)
                return carry

            lax.fori_loop(0, 2 * dates, clear, 0)

    def shift(i, carry):
        s = i // dates

        @pl.when((i % PACE) == 0)
        def _():
            slot(1 + i // PACE)

        @pl.when(i == (rows - 2) * dates)
        def _():
            for k in range(2):
                fringe(k)

        p = jnp.where(s < rows - 2, s + 1, jnp.where(s == rows - 2, 0, rows - 1))
        resample(p, i % dates, sizes, at_ref, ct_ref, pr_ref, wide, shifted, devs, stats)
        return carry

    lax.fori_loop(0, dates * rows, shift, 0)

    @pl.when(mine == 0)
    def _():
        own.wait()

    begun = 1 + -(-dates * rows // PACE)
    last = pieces + max(0, count - 3) * LAG

    def window_of(g):
        return (g * (8 * LOOK_AZ) + 8 * LOOK_AZ - 1) // WIN

    def due(g):
        ready = jnp.minimum(last, (window_of(g) + 1) * each + (count - 2) * LAG)
        return jnp.where(g < 0, begun, jnp.maximum(begun, ready))

    def group(g):
        p = window_of(g)

        def forward(t, carry):
            slot(t)
            return carry

        lax.fori_loop(due(g - 1), due(g), forward, 0)

        @pl.when((g == 0) | (p > window_of(g - 1)))
        def _():
            for c in range(2):
                @pl.when(hops[c] == count - 1)
                def _():
                    for e in range(each):
                        relay(c, p * each + e, False).wait_recv()

            prepare(p, sizes, ref, ref32, devs, stats)
            similarity(p, sizes, blk_ref, stats, sim_ref)

        interferogram(g, sizes, rgp_ref, ref32, shifted, prod, pooled)

    def patches(h, carry):
        share = groups // halves

        def one(i, inner):
            group(h * share + i)
            return inner

        lax.fori_loop(0, share, one, 0)
        goldstein(h, dates, out_ref, dft_ref, blk_ref, pooled)
        return carry

    lax.fori_loop(0, halves, patches, 0)

    for c in range(2):
        @pl.when(hops[c] < count - 1)
        def _():
            def drain(j, carry):
                relay(c, j, False).wait_send()
                return carry

            lax.fori_loop(0, pieces, drain, 0)

    for k in range(2):
        @pl.when(sends[k])
        def _():
            edge(k).wait_send()


def on_device(image, along, cross, present):
    dates, _, lines, samples = image.shape
    strips = samples // LANES
    rows = lines // WIN
    pieces = lines // PIECE
    halves = lines // (LOOK_AZ * PATCH)
    smem = pl.BlockSpec(memory_space=pltpu.SMEM)
    vmem = pl.BlockSpec(memory_space=pltpu.VMEM)
    dma = pltpu.SemaphoreType.DMA
    dft, blocks, rg_pool = tables(samples)
    found, filtered = pl.pallas_call(
        kernel,
        out_shape=(
            jax.ShapeDtypeStruct((rows, dates, samples // WIN), F32),
            jax.ShapeDtypeStruct((dates, 2, lines // LOOK_AZ, samples // LOOK_RG), F32),
        ),
        in_specs=[smem] * 3 + [pl.BlockSpec(memory_space=pl.ANY)] + [vmem] * 3,
        out_specs=(vmem, vmem),
        scratch_shapes=[
            pltpu.VMEM((dates, 2, lines, samples), BF16),
            pltpu.VMEM((2, dates, 2, MARGIN, samples), BF16),
            pltpu.VMEM((2, lines, samples), BF16),
            pltpu.VMEM((dates, 2, strips, lines + 2 * MARGIN + WIN, LANES), F32),
            pltpu.VMEM((dates, 2, strips, lines, LANES), F32),
            pltpu.VMEM((dates, strips, lines, LANES), F32),
            pltpu.VMEM((2, strips, lines, LANES), F32),
            pltpu.VMEM((2, dates, 16, samples), BF16),
            pltpu.VMEM((halves, dates // 2, 2, 2, PATCH, samples // LOOK_RG), F32),
            pltpu.VMEM((rows, 3, strips, dates + 1, 8, LANES), F32),
            dma((2 * dates,)),
            dma(()),
            dma((2,)),
            dma((2,)),
            dma((2, pieces)),
            dma((2, pieces)),
        ],
        compiler_params=pltpu.CompilerParams(
            vmem_limit_bytes=62 * 1024 * 1024, collective_id=0, has_side_effects=True
        ),
    )(
        along.transpose(1, 0, 2), cross.transpose(1, 0, 2), present, image, dft, blocks, rg_pool
    )
    return found.transpose(1, 0, 2), filtered


def solution(mesh):
    placed = (
        P("date", None, "az", None),
        P("date", "az", None),
        P("date", "az", None),
        P("date", "az"),
    )
    return jax.shard_map(
        on_device,
        mesh=mesh,
        in_specs=placed,
        out_specs=(P("date", "az", None), P("date", None, "az", None)),
        check_vma=False,
    )
```

time: 41.4 us -> 45.1 us (1.089)
  local copies, waits for them, and re-layouts: 0 us -> 2.97 us
  Pallas kernels: 40.6 us -> 41.2 us
    pallas_call x1, Pallas kernels: 36.2 us -> 41.2 us  [on_device(): pl.pallas_call(kernel, out_shape=(jax.ShapeDtypeStruct((rows, dates, samp...]
    pallas_call x1 -> x0, Pallas kernels: 4.44 us -> none  [on_device(): pl.pallas_call(finish, out_shape=(jax.ShapeDtypeStruct(similarity.shape,...]
    unnamed x0 -> x2, local copies, waits for them, and re-layouts: none -> 2.97 us
where the time goes in v1:
time: 45.1 us; the launch traced here: 44.8 us
  Pallas kernels  41.2 us (91%)
  local copies, waits for them, and re-layouts  2.97 us (7%)
  between operations  0.64 us (1%)
    pallas_call x1, Pallas kernels, on_device(): pl.pallas_call(kernel, out_shape=(jax.ShapeDtypeStruct((rows, dates, samp...  41.2 us
    unnamed x2, local copies, waits for them, and re-layouts  2.97 us

profile of v1, /device:TPU:10, one launch (start us, length us, event | category | flops | bytes accessed | tf_op | source)
XLA Modules:
  0.0 44.8 jit_solution(17542233058698263829)
XLA Ops:
  0.6 41.2 %shard_map.86 = (f32[5,4,20]{2,1,0:T(4,128)}, f32[4,2,64,64]{3,2,1,0:T(8,128)}) custom-call(s32[5,4,20]{2,1,0:T(4,128)} %bitcast.3, s32[5,4,20]{2,1,0:T(4,128)} %bitcast.4, s32[4,5]{1,0:T(4,128)} %pr_ref.1, bf16[4,2,320,1280]{3,2,1,0:T(8,128)(2,1)} %img_ref.1, f32[2,128,128]{2,1,0:T(8,128)} %constant.6.clone.dft_ref, ...), custom_call_target="tpu_custom_call" | custom-call | tf_op jit(solution)/shard_map/pallas_call | solution.py:461
  41.9 1.3 %copy.11 = f32[4,5,20]{2,0,1:T(4,128)} copy(f32[4,5,20]{2,0,1:T(4,128)} %bitcast.5) | data formatting | bytes 3200
  43.2 1.7 %copy.12 = f32[4,2,64,64]{3,2,1,0:T(8,128)} copy(f32[4,2,64,64]{3,2,1,0:T(8,128)} %get-tuple-element.9) | data formatting | bytes 262144

commit v2 on v1

--- a/solution.py
+++ b/solution.py
@@ -15,6 +15,8 @@
 PIECE = 16
 LAG = 3
 PACE = 3
+HALO_SLOT = 9
+DUP = 3
 
 VAR_EPS = 1e-05
 RMS_EPS = 1e-06
@@ -180,7 +182,7 @@
     at = pl.ds(pl.multiple_of((g % groups) * 8, 8), 8)
     for d in range(dates):
         for c in range(2):
-            pooled[g // groups, d // 2, c, d % 2, at, :] = sums[d, c]
+            pooled[d // 2, c, d % 2, at, :] = sums[d, c]
 
 
 def goldstein(h, dates, out_ref, dft_ref, blk_ref, pooled):
@@ -193,7 +195,7 @@
 
     turned = []
     for e in range(pairs):
-        z = pooled[h, e].reshape(2 * WIN, -1)
+        z = pooled[e].reshape(2 * WIN, -1)
         turned.append(rows_to_cols(dot_high(rows_fwd, z)))
     spectrum = dot_high(jnp.concatenate(turned, axis=0), cols_fwd)
     squares = spectrum * spectrum
@@ -205,16 +207,17 @@
         + jnp.concatenate([smooth[:, -1:], smooth[:, :-1]], axis=1)
     ).reshape(spectrum.shape)
     weighted = spectrum * root(smooth * (1.0 / 9.0))
+    squares = weighted * weighted
+    power = jnp.sum((squares + pltpu.roll(squares, WIN, 1)).reshape(-1, PATCH // 8, 8, LANES), axis=1)
+    power = dot_right(power.reshape(-1, LANES), blk_ref[2]).reshape(-1, 8, LANES)
+    scale = lax.rsqrt(jnp.sum(power, axis=1, keepdims=True) + RMS_EPS)
     turned = []
     for e in range(pairs):
         w = weighted[e * WIN : (e + 1) * WIN]
         w = jnp.concatenate([w[:, :WIN], w[:, WIN:]], axis=0)
         turned.append(rows_to_cols(dot_high(cols_fwd, w)))
     back = dot_high(jnp.concatenate(turned, axis=0), rows_fwd)
-    squares = back * back
-    power = dot_right(squares + pltpu.roll(squares, WIN, 1), blk_ref[2]).reshape(-1, PATCH, LANES)
-    power = jnp.sum(power, axis=1, keepdims=True) * (1.0 / (PATCH * PATCH))
-    scaled = back.reshape(-1, PATCH, LANES) * lax.rsqrt(power + RMS_EPS)
+    scaled = back.reshape(-1, PATCH, LANES) * scale
     at = pl.ds(pl.multiple_of(h * PATCH, PATCH), PATCH)
     for d in range(dates):
         out_ref[d, 0, at, :] = scaled[d][:, :WIN]
@@ -227,10 +230,11 @@
 
 
 def kernel(
-    at_ref, ct_ref, pr_ref, img_ref, dft_ref, blk_ref, rgp_ref,
-    sim_ref, out_ref,
-    image, halo, ref, wide, shifted, devs, ref32, prod, pooled, stats,
-    image_sem, root_sem, halo_send, halo_recv, ref_send, ref_recv,
+    at_hbm, ct_hbm, pr_hbm, img_ref, dft_hbm, blk_hbm, rgp_hbm,
+    sim_ref, out_ref, pooled,
+    image, halo, ref, wide, shifted, devs, ref32, prod, stats,
+    at_ref, ct_ref, pr_ref, dft_ref, blk_ref, rgp_ref,
+    image_sem, root_sem, table_sem, halo_send, halo_recv, ref_send, ref_recv, dup_send,
 ):
     dates, _, lines, samples = img_ref.shape
     strips = samples // LANES
@@ -259,6 +263,13 @@
 
     for i in range(2 * dates):
         load(i).start()
+    pairs = (
+        (at_hbm, at_ref), (ct_hbm, ct_ref), (pr_hbm, pr_ref),
+        (dft_hbm, dft_ref), (blk_hbm, blk_ref), (rgp_hbm, rgp_ref),
+    )
+    extras = [pltpu.make_async_copy(a, b, table_sem.at[i]) for i, (a, b) in enumerate(pairs)]
+    for copy in extras:
+        copy.start()
     own = pltpu.make_async_copy(img_ref.at[0], ref, root_sem)
 
     @pl.when(mine == 0)
@@ -291,6 +302,19 @@
             device_id_type=mesh_ids,
         )
 
+    dups = DUP if count > 2 else 0
+
+    def direct(c, e):
+        at = pl.ds(lines - (dups - e) * height, height)
+        return pltpu.make_async_remote_copy(
+            src_ref=img_ref.at[0, c, at],
+            dst_ref=ref.at[c, at],
+            send_sem=dup_send.at[c, e],
+            recv_sem=ref_recv.at[c, pieces - dups + e],
+            device_id={"date": targets[1 - c]},
+            device_id_type=mesh_ids,
+        )
+
     @pl.when(mine == 0)
     def _():
         def launch(j, carry):
@@ -299,14 +323,25 @@
             return carry
 
         lax.fori_loop(0, pieces, launch, 0)
+        for e in range(dups):
+            for c in range(2):
+                direct(c, e).start()
+
+    def sent(c):
+        return jnp.where(hops[c] == count - 2, pieces - dups, jnp.where(hops[c] == count - 1, 0, pieces))
 
     def slot(t):
         for c in range(2):
             j = t - (hops[c] - 1) * LAG
 
-            @pl.when((hops[c] > 0) & (hops[c] < count - 1) & (j >= 0) & (j < pieces))
+            here = (hops[c] > 0) & (hops[c] < count - 1) & (j >= 0) & (j < pieces)
+
+            @pl.when(here)
             def _():
                 relay(c, j, False).wait_recv()
+
+            @pl.when(here & (j < sent(c)))
+            def _():
                 relay(c, j, False).start()
 
     def edge(k):
@@ -366,46 +401,55 @@
 
             lax.fori_loop(0, 2 * dates, clear, 0)
 
-    def shift(i, carry):
-        s = i // dates
-
-        @pl.when((i % PACE) == 0)
-        def _():
-            slot(1 + i // PACE)
-
-        @pl.when(i == (rows - 2) * dates)
-        def _():
-            for k in range(2):
-                fringe(k)
-
-        p = jnp.where(s < rows - 2, s + 1, jnp.where(s == rows - 2, 0, rows - 1))
-        resample(p, i % dates, sizes, at_ref, ct_ref, pr_ref, wide, shifted, devs, stats)
+    for copy in extras[:3]:
+        copy.wait()
+
+    def forward(t, carry):
+        slot(t)
         return carry
 
-    lax.fori_loop(0, dates * rows, shift, 0)
+    def shift(first, begin):
+        def one(i, carry):
+            @pl.when((i % PACE) == 0)
+            def _():
+                slot(first + i // PACE)
+
+            s = begin + i // dates
+            p = jnp.where(s < rows - 2, s + 1, jnp.where(s == rows - 2, 0, rows - 1))
+            resample(p, i % dates, sizes, at_ref, ct_ref, pr_ref, wide, shifted, devs, stats)
+            return carry
+
+        return one
+
+    inner = dates * (rows - 2)
+    lax.fori_loop(0, inner, shift(1, 0), 0)
+    lax.fori_loop(1 + -(-inner // PACE), HALO_SLOT, forward, 0)
+    for k in range(2):
+        fringe(k)
+    lax.fori_loop(0, 2 * dates, shift(HALO_SLOT, rows - 2), 0)
 
     @pl.when(mine == 0)
     def _():
         own.wait()
 
-    begun = 1 + -(-dates * rows // PACE)
+    for copy in extras[3:]:
+        copy.wait()
+
+    begun = HALO_SLOT + -(-2 * dates // PACE)
     last = pieces + max(0, count - 3) * LAG
 
     def window_of(g):
         return (g * (8 * LOOK_AZ) + 8 * LOOK_AZ - 1) // WIN
 
-    def due(g):
-        ready = jnp.minimum(last, (window_of(g) + 1) * each + (count - 2) * LAG)
-        return jnp.where(g < 0, begun, jnp.maximum(begun, ready))
+    def due(g, after):
+        p = window_of(g)
+        ready = jnp.maximum((p + 1) * each + (count - 2) * LAG, begun + 1 + g + p + after)
+        return jnp.where(g < 0, begun, jnp.minimum(last, ready))
 
     def group(g):
         p = window_of(g)
 
-        def forward(t, carry):
-            slot(t)
-            return carry
-
-        lax.fori_loop(due(g - 1), due(g), forward, 0)
+        lax.fori_loop(due(g - 1, 1), due(g, 0), forward, 0)
 
         @pl.when((g == 0) | (p > window_of(g - 1)))
         def _():
@@ -418,6 +462,7 @@
             prepare(p, sizes, ref, ref32, devs, stats)
             similarity(p, sizes, blk_ref, stats, sim_ref)
 
+        lax.fori_loop(due(g, 0), due(g, 1), forward, 0)
         interferogram(g, sizes, rgp_ref, ref32, shifted, prod, pooled)
 
     def patches(h, carry):
@@ -428,7 +473,11 @@
             return inner
 
         lax.fori_loop(0, share, one, 0)
-        goldstein(h, dates, out_ref, dft_ref, blk_ref, pooled)
+
+        @pl.when(h < halves - 1)
+        def _():
+            goldstein(h, dates, out_ref, dft_ref, blk_ref, pooled)
+
         return carry
 
     lax.fori_loop(0, halves, patches, 0)
@@ -440,12 +489,25 @@
                 relay(c, j, False).wait_send()
                 return carry
 
-            lax.fori_loop(0, pieces, drain, 0)
+            lax.fori_loop(0, sent(c), drain, 0)
+
+    @pl.when(mine == 0)
+    def _():
+        for e in range(dups):
+            for c in range(2):
+                direct(c, e).wait_send()
 
     for k in range(2):
         @pl.when(sends[k])
         def _():
             edge(k).wait_send()
+
+
+def finish(found_ref, early_ref, pooled_ref, dft_ref, blk_ref, sim_ref, out_ref):
+    dates, _, early, _ = early_ref.shape
+    sim_ref[...] = found_ref[...]
+    out_ref[:, :, :early] = early_ref[...]
+    goldstein(early // PATCH, dates, out_ref, dft_ref, blk_ref, pooled_ref)
 
 
 def on_device(image, along, cross, present):
@@ -454,18 +516,19 @@
     rows = lines // WIN
     pieces = lines // PIECE
     halves = lines // (LOOK_AZ * PATCH)
-    smem = pl.BlockSpec(memory_space=pltpu.SMEM)
+    looks = samples // LOOK_RG
     vmem = pl.BlockSpec(memory_space=pltpu.VMEM)
     dma = pltpu.SemaphoreType.DMA
     dft, blocks, rg_pool = tables(samples)
-    found, filtered = pl.pallas_call(
+    found, early, pooled = pl.pallas_call(
         kernel,
         out_shape=(
             jax.ShapeDtypeStruct((rows, dates, samples // WIN), F32),
-            jax.ShapeDtypeStruct((dates, 2, lines // LOOK_AZ, samples // LOOK_RG), F32),
+            jax.ShapeDtypeStruct((dates, 2, (halves - 1) * PATCH, looks), F32),
+            jax.ShapeDtypeStruct((dates // 2, 2, 2, PATCH, looks), F32),
         ),
-        in_specs=[smem] * 3 + [pl.BlockSpec(memory_space=pl.ANY)] + [vmem] * 3,
-        out_specs=(vmem, vmem),
+        in_specs=[pl.BlockSpec(memory_space=pl.ANY)] * 7,
+        out_specs=(vmem, vmem, vmem),
         scratch_shapes=[
             pltpu.VMEM((dates, 2, lines, samples), BF16),
             pltpu.VMEM((2, dates, 2, MARGIN, samples), BF16),
@@ -475,14 +538,21 @@
             pltpu.VMEM((dates, strips, lines, LANES), F32),
             pltpu.VMEM((2, strips, lines, LANES), F32),
             pltpu.VMEM((2, dates, 16, samples), BF16),
-            pltpu.VMEM((halves, dates // 2, 2, 2, PATCH, samples // LOOK_RG), F32),
             pltpu.VMEM((rows, 3, strips, dates + 1, 8, LANES), F32),
+            pltpu.SMEM((rows, dates, samples // WIN), jnp.int32),
+            pltpu.SMEM((rows, dates, samples // WIN), jnp.int32),
+            pltpu.SMEM((dates, rows), jnp.int32),
+            pltpu.VMEM(dft.shape, F32),
+            pltpu.VMEM(blocks.shape, BF16),
+            pltpu.VMEM(rg_pool.shape, BF16),
             dma((2 * dates,)),
             dma(()),
+            dma((6,)),
             dma((2,)),
             dma((2,)),
             dma((2, pieces)),
             dma((2, pieces)),
+            dma((2, DUP)),
         ],
         compiler_params=pltpu.CompilerParams(
             vmem_limit_bytes=62 * 1024 * 1024, collective_id=0, has_side_effects=True
@@ -490,6 +560,15 @@
     )(
         along.transpose(1, 0, 2), cross.transpose(1, 0, 2), present, image, dft, blocks, rg_pool
     )
+    found, filtered = pl.pallas_call(
+        finish,
+        out_shape=(
+            jax.ShapeDtypeStruct(found.shape, F32),
+            jax.ShapeDtypeStruct((dates, 2, lines // LOOK_AZ, looks), F32),
+        ),
+        in_specs=[vmem] * 5,
+        out_specs=(vmem, vmem),
+    )(found, early, pooled, dft, blocks)
     return found.transpose(1, 0, 2), filtered
 
 

time: 45.1 us -> 35 us (0.78)
  Pallas kernels: 41.2 us -> 33.7 us
  local copies, waits for them, and re-layouts: 2.97 us -> 0 us
    pallas_call x1, Pallas kernels: 41.2 us -> 30.6 us  [on_device(): pl.pallas_call(kernel, out_shape=(jax.ShapeDtypeStruct((rows, dates, samp...]
    pallas_call x0 -> x1, Pallas kernels: none -> 3.07 us  [on_device(): pl.pallas_call(finish, out_shape=(jax.ShapeDtypeStruct(found.shape, F32),...]
    unnamed x2 -> x0, local copies, waits for them, and re-layouts: 2.97 us -> none
where the time goes in v2:
time: 35 us; the launch traced here: 34.3 us
  Pallas kernels  33.7 us (96%)
  between operations  0.64 us (2%)
    pallas_call x1, Pallas kernels, on_device(): pl.pallas_call(kernel, out_shape=(jax.ShapeDtypeStruct((rows, dates, samp...  30.6 us
    pallas_call x1, Pallas kernels, on_device(): pl.pallas_call(finish, out_shape=(jax.ShapeDtypeStruct(found.shape, F32),...  3.07 us

profile of v2, /device:TPU:10, one launch (start us, length us, event | category | flops | bytes accessed | tf_op | source)
XLA Modules:
  0.0 34.3 jit_solution(4647806424536760660)
XLA Ops:
  0.6 30.6 %shard_map.86 = (f32[5,4,20]{2,1,0:T(4,128)}, f32[4,2,32,64]{3,2,1,0:T(8,128)}, f32[2,2,2,32,64]{4,3,2,1,0:T(8,128)}) custom-call(s32[5,4,20]{2,1,0:T(4,128)} %bitcast.3, s32[5,4,20]{2,1,0:T(4,128)} %bitcast.4, s32[4,5]{1,0:T(4,128)} %pr_hbm.1, bf16[4,2,320,1280]{3,2,1,0:T(8,128)(2,1)} %img_ref.1, f32[2,128,128]{2,1,0:T(8,128)} %constant.6.clone.dft_hbm.dft_ref, ...), custom_call_target="tpu_custom_call" | custom-call | tf_op jit(solution)/shard_map/pallas_call | solution.py:523
  31.2 3.1 %shard_map.87 = (f32[5,4,20]{2,1,0:T(4,128)}, f32[4,2,64,64]{3,2,1,0:T(8,128)}) custom-call(f32[5,4,20]{2,1,0:T(4,128)} %get-tuple-element.7.found_ref, f32[4,2,32,64]{3,2,1,0:T(8,128)} %get-tuple-element.8.early_ref, f32[2,2,2,32,64]{4,3,2,1,0:T(8,128)} %get-tuple-element.9.pooled_ref, f32[2,128,128]{2,1,0:T(8,128)} %constant.6.clone.dft_hbm.dft_ref, ...), custom_call_target="tpu_custom_call" | custom-call | tf_op jit(solution)/shard_map/pallas_call | solution.py:563

commit v3 on v2

--- a/solution.py
+++ b/solution.py
@@ -1,5 +1,6 @@
 import jax
 import jax.numpy as jnp
+import ml_dtypes
 import numpy as np
 from jax import lax
 from jax.experimental import pallas as pl
@@ -13,9 +14,9 @@
 PATCH = 32
 LANES = 128
 PIECE = 16
-LAG = 3
-PACE = 3
-HALO_SLOT = 9
+LAG = 4
+PACE = 2
+HALO_SLOT = 12
 DUP = 3
 
 VAR_EPS = 1e-05
@@ -26,40 +27,39 @@
 BF16 = jnp.bfloat16
 
 
-def tables(samples):
+def two_terms(x):
+    x = x.astype(np.float32)
+    high = x.astype(ml_dtypes.bfloat16)
+    return high, (x - high.astype(np.float32)).astype(ml_dtypes.bfloat16)
+
+
+def tables(dates, samples):
     turns = np.outer(np.arange(PATCH), np.arange(PATCH)) % PATCH
     angles = turns * (2.0 * np.pi / PATCH)
-    two = np.eye(2)
+    two = np.eye(samples // LOOK_RG // PATCH)
     cosine = np.kron(two, np.cos(angles))
     sine = np.kron(two, np.sin(angles))
-    rows_fwd = np.block([[cosine, sine], [-sine, cosine]])
-    cols_fwd = np.block([[cosine, -sine], [sine, cosine]])
-    dft = np.stack([rows_fwd, cols_fwd]).astype(np.float32)
+    each = np.eye(dates)
+    left = np.concatenate([np.kron(each, np.cos(angles)), np.kron(each, np.sin(angles))], axis=1)
+    right = np.block([[cosine, sine], [-sine, cosine]])
     near = np.abs(np.arange(PATCH)[:, None] - np.arange(PATCH)[None, :])
     circular = np.minimum(near, PATCH - near) <= 1
     four = np.eye(LANES // PATCH)
     half = np.kron(np.eye(2), np.ones((WIN, WIN)))
-    blocks = np.stack(
-        [half, np.kron(four, circular), np.kron(four, np.ones((PATCH, PATCH)))]
-    ).astype(np.float32)
-    rg_pool = (
-        np.arange(samples)[:, None] // LOOK_RG == np.arange(samples // LOOK_RG)[None, :]
-    ).astype(np.float32)
+    blocks = np.stack([half, np.kron(four, circular), np.kron(four, np.ones((PATCH, PATCH)))])
+    blocks = np.concatenate([blocks, blocks], axis=1)
+    pool = np.arange(samples)[:, None] // LOOK_RG == np.arange(samples // LOOK_RG)[None, :]
+    pool = pool.astype(np.float64) @ np.concatenate([cosine, -sine], axis=1)
     return (
-        jnp.asarray(dft),
+        jnp.asarray(np.stack(two_terms(left))),
+        jnp.asarray(np.concatenate(two_terms(right), axis=1)),
         jnp.asarray(blocks, BF16),
-        jnp.asarray(rg_pool, BF16),
+        jnp.asarray(np.concatenate(two_terms(pool), axis=1)),
     )
 
 
 def dot(a, b):
     return jnp.dot(a, b, preferred_element_type=F32)
-
-
-def dot_high(a, b):
-    a_high, a_low = split(a)
-    b_high, b_low = split(b)
-    return dot(a_high, b_high) + (dot(a_high, b_low) + dot(a_low, b_high))
 
 
 def split(x):
@@ -68,8 +68,11 @@
 
 
 def dot_right(x, ones):
-    high, low = split(x)
-    return dot(high, ones) + dot(low, ones)
+    return dot(jnp.concatenate(split(x), axis=1), ones)
+
+
+def turned(x, sign):
+    return sign * pltpu.roll(x, WIN, 1)
 
 
 def root(x):
@@ -111,43 +114,57 @@
         stats[p, 1, m, d] = jnp.sum(dev * dev, axis=0)
 
 
-def prepare(p, sizes, ref, ref32, devs, stats):
+def total(x, half):
+    sums = dot_right(x.reshape(-1, LANES), half).reshape(-1, 8, LANES)
+    return jnp.sum(sums, axis=1, keepdims=True)
+
+
+def settle(p, sizes, blk_ref, stats):
     dates, lines, strips = sizes
-    here = pl.ds(pl.multiple_of(p * WIN, WIN), WIN)
+    half = blk_ref[0]
+    shape = (strips * dates, 8, LANES)
+    means = stats[p, 0].reshape(shape)
+    away = means - total(means, half) * (1.0 / (8.0 * WIN))
+    spread = stats[p, 1].reshape(shape) + (WIN / 8.0) * (away * away)
+    var = total(spread, half) * (1.0 / (WIN * WIN))
+    stats[p, 0] = away.reshape(strips, dates, 8, LANES)
+    stats[p, 1] = jnp.broadcast_to(var + VAR_EPS, shape).reshape(strips, dates, 8, LANES)
+
+
+def prepare(p, e, height, sizes, ref, ref32, devs, stats, own):
+    dates, lines, strips = sizes
+    here = pl.ds(pl.multiple_of(p * WIN + e * height, height), height)
+    fresh = e == 0
     for m in range(strips):
         cols = slice(m * LANES, (m + 1) * LANES)
         real = ref[0, here, cols].astype(F32)
         imag = ref[1, here, cols].astype(F32)
         ref32[0, m, here, :] = real
         ref32[1, m, here, :] = imag
-        amp = root(real * real + imag * imag).reshape(WIN // 8, 8, LANES)
-        mean = jnp.sum(amp, axis=0) * (8.0 / WIN)
-        dev = amp - mean[None]
-        stats[p, 0, m, dates] = mean
-        stats[p, 1, m, dates] = jnp.sum(dev * dev, axis=0)
+        amp = root(real * real + imag * imag).reshape(height // 8, 8, LANES)
+        pivot = jnp.where(fresh, amp[0], own[p, 0, m])
+        own[p, 0, m] = pivot
+        dev = amp - pivot[None]
+        own[p, 1, m] = jnp.sum(dev, axis=0) + jnp.where(fresh, 0.0, own[p, 1, m])
+        own[p, 2, m] = jnp.sum(dev * dev, axis=0) + jnp.where(fresh, 0.0, own[p, 2, m])
         for d in range(dates):
-            joint = devs[d, m, here, :].reshape(WIN // 8, 8, LANES) * dev
-            stats[p, 2, m, d] = jnp.sum(joint, axis=0)
-
-
-def similarity(p, sizes, blk_ref, stats, sim_ref):
+            joint = devs[d, m, here, :].reshape(height // 8, 8, LANES) * dev
+            stats[p, 2, m, d] = jnp.sum(joint, axis=0) + jnp.where(fresh, 0.0, stats[p, 2, m, d])
+
+
+def similarity(p, sizes, blk_ref, stats, own, sim_ref):
     dates, lines, strips = sizes
     half = blk_ref[0]
-
-    def total(x):
-        flat = x.reshape(-1, LANES)
-        return jnp.sum(dot_right(flat, half).reshape(-1, 8, LANES), axis=1, keepdims=True)
-
-    count = 8.0 * WIN
-    means = stats[p, 0].reshape(strips * (dates + 1), 8, LANES)
-    away = means - total(means) * (1.0 / count)
-    spread = stats[p, 1].reshape(strips * (dates + 1), 8, LANES)
-    var = total(spread + (WIN / 8.0) * (away * away)) * (1.0 / (WIN * WIN))
-    away = away.reshape(strips, dates + 1, 8, LANES)
-    var = var.reshape(strips, dates + 1, 1, LANES)
-    joint = stats[p, 2][:, :dates] + (WIN / 8.0) * (away[:, :dates] * away[:, dates:])
-    cov = total(joint).reshape(strips, dates, 1, LANES) * (1.0 / (WIN * WIN))
-    corr = cov / jnp.sqrt((var[:, dates:] + VAR_EPS) * (var[:, :dates] + VAR_EPS))
+    first = own[p, 1]
+    means = own[p, 0] + first * (8.0 / WIN)
+    away = means - total(means, half) * (1.0 / (8.0 * WIN))
+    spread = own[p, 2] - first * first * (8.0 / WIN) + (WIN / 8.0) * (away * away)
+    joint = stats[p, 2] + (WIN / 8.0) * (stats[p, 0] * away[:, None])
+    every = jnp.concatenate([spread, joint.reshape(strips * dates, 8, LANES)], axis=0)
+    every = total(every, half) * (1.0 / (WIN * WIN))
+    var = every[:strips].reshape(strips, 1, 1, LANES)
+    cov = every[strips:].reshape(strips, dates, 1, LANES)
+    corr = cov * lax.rsqrt((var + VAR_EPS) * stats[p, 1][:, :, :1])
     lane = lax.broadcasted_iota(jnp.int32, (dates, 1, LANES), 2)
     found = jnp.zeros((dates, 1, LANES), F32)
     for m in range(strips):
@@ -159,45 +176,49 @@
     sim_ref[p] = found.reshape(dates, LANES)[:, : sim_ref.shape[2]]
 
 
-def interferogram(g, sizes, rgp_ref, ref32, shifted, prod, pooled):
+def interferogram(g, sizes, rgp_ref, ref32, shifted, pooled):
     dates, lines, strips = sizes
     rows = [pl.ds(g * (8 * LOOK_AZ) + k, 8, stride=LOOK_AZ) for k in range(LOOK_AZ)]
-    for m in range(strips):
-        cols = slice(m * LANES, (m + 1) * LANES)
-        rr = [ref32[0, m, at, :] for at in rows]
-        ri = [ref32[1, m, at, :] for at in rows]
-        for d in range(dates):
-            real = imag = 0.0
-            for k, at in enumerate(rows):
-                sr = shifted[d, 0, m, at, :]
-                si = shifted[d, 1, m, at, :]
-                real = real + (rr[k] * sr + ri[k] * si)
-                imag = imag + (ri[k] * sr - rr[k] * si)
-            high, low = split(jnp.concatenate([real, imag], axis=0))
-            prod[0, d, :, cols] = high
-            prod[1, d, :, cols] = low
-    sums = dot(prod[...].reshape(2 * dates * 16, strips * LANES), rgp_ref[...])
-    sums = (sums[: dates * 16] + sums[dates * 16 :]).reshape(dates, 2, 8, -1)
-    groups = PATCH // 8
-    at = pl.ds(pl.multiple_of((g % groups) * 8, 8), 8)
+    sums = 0.0
+    for base in range(0, strips, 2):
+        terms = []
+        for m in range(base, min(base + 2, strips)):
+            rr = [ref32[0, m, at, :] for at in rows]
+            ri = [ref32[1, m, at, :] for at in rows]
+            column = []
+            for d in range(dates):
+                real = imag = 0.0
+                for k, at in enumerate(rows):
+                    sr = shifted[d, 0, m, at, :]
+                    si = shifted[d, 1, m, at, :]
+                    real = real + (rr[k] * sr + ri[k] * si)
+                    imag = imag + (ri[k] * sr - rr[k] * si)
+                column.append(jnp.concatenate([real, imag], axis=0))
+            terms.append(split(jnp.concatenate(column, axis=0)))
+        width = len(terms) * LANES
+        lhs = jnp.concatenate(
+            [jnp.concatenate([t[k] for t in terms], axis=1) for k in range(2)], axis=0
+        )
+        sums = sums + dot(lhs, rgp_ref[base * LANES : base * LANES + width])
+    high = sums[: dates * 16]
+    sums = high[:, :LANES] + (high[:, LANES:] + sums[dates * 16 :, :LANES])
+    sums = sums.reshape(dates, 2, 8, LANES)
+    sign = jnp.where(lax.broadcasted_iota(jnp.int32, (8, LANES), 1) < WIN, -1.0, 1.0)
+    at = pl.ds(pl.multiple_of((g % (PATCH // 8)) * 8, 8), 8)
     for d in range(dates):
-        for c in range(2):
-            pooled[d // 2, c, d % 2, at, :] = sums[d, c]
-
-
-def goldstein(h, dates, out_ref, dft_ref, blk_ref, pooled):
-    rows_fwd = dft_ref[0]
-    cols_fwd = dft_ref[1]
-    pairs = dates // 2
-
-    def rows_to_cols(x):
-        return jnp.concatenate([x[:WIN], x[WIN:]], axis=1)
-
-    turned = []
-    for e in range(pairs):
-        z = pooled[e].reshape(2 * WIN, -1)
-        turned.append(rows_to_cols(dot_high(rows_fwd, z)))
-    spectrum = dot_high(jnp.concatenate(turned, axis=0), cols_fwd)
+        pooled[d, at, :] = sums[d, 0] + turned(sums[d, 1], sign)
+
+
+def goldstein(h, dates, out_ref, left_ref, right_ref, blk_ref, pooled):
+    count = dates * PATCH
+    sign = jnp.where(lax.broadcasted_iota(jnp.int32, (count, LANES), 1) < WIN, -1.0, 1.0)
+
+    def down(x, sign):
+        high, low = split(jnp.concatenate([x, turned(x, sign)], axis=0))
+        both = dot(left_ref[0], jnp.concatenate([high, low], axis=1))
+        return both[:, :LANES] + (both[:, LANES:] + dot(left_ref[1], high))
+
+    spectrum = down(pooled[...].reshape(count, LANES), -sign)
     squares = spectrum * spectrum
     magnitude = root(squares + pltpu.roll(squares, WIN, 1))
     smooth = dot_right(magnitude, blk_ref[1]).reshape(-1, PATCH, LANES)
@@ -211,12 +232,9 @@
     power = jnp.sum((squares + pltpu.roll(squares, WIN, 1)).reshape(-1, PATCH // 8, 8, LANES), axis=1)
     power = dot_right(power.reshape(-1, LANES), blk_ref[2]).reshape(-1, 8, LANES)
     scale = lax.rsqrt(jnp.sum(power, axis=1, keepdims=True) + RMS_EPS)
-    turned = []
-    for e in range(pairs):
-        w = weighted[e * WIN : (e + 1) * WIN]
-        w = jnp.concatenate([w[:, :WIN], w[:, WIN:]], axis=0)
-        turned.append(rows_to_cols(dot_high(cols_fwd, w)))
-    back = dot_high(jnp.concatenate(turned, axis=0), rows_fwd)
+    high, low = split(down(weighted, sign))
+    both = dot(high, right_ref[...])
+    back = both[:, :LANES] + (both[:, LANES:] + dot(low, right_ref[:, :LANES]))
     scaled = back.reshape(-1, PATCH, LANES) * scale
     at = pl.ds(pl.multiple_of(h * PATCH, PATCH), PATCH)
     for d in range(dates):
@@ -230,10 +248,10 @@
 
 
 def kernel(
-    at_hbm, ct_hbm, pr_hbm, img_ref, dft_hbm, blk_hbm, rgp_hbm,
+    at_hbm, ct_hbm, pr_hbm, img_ref, left_hbm, right_hbm, blk_hbm, rgp_hbm,
     sim_ref, out_ref, pooled,
-    image, halo, ref, wide, shifted, devs, ref32, prod, stats,
-    at_ref, ct_ref, pr_ref, dft_ref, blk_ref, rgp_ref,
+    image, halo, ref, wide, shifted, devs, ref32, stats, root_stats,
+    at_ref, ct_ref, pr_ref, left_ref, right_ref, blk_ref, rgp_ref,
     image_sem, root_sem, table_sem, halo_send, halo_recv, ref_send, ref_recv, dup_send,
 ):
     dates, _, lines, samples = img_ref.shape
@@ -265,7 +283,7 @@
         load(i).start()
     pairs = (
         (at_hbm, at_ref), (ct_hbm, ct_ref), (pr_hbm, pr_ref),
-        (dft_hbm, dft_ref), (blk_hbm, blk_ref), (rgp_hbm, rgp_ref),
+        (left_hbm, left_ref), (right_hbm, right_ref), (blk_hbm, blk_ref), (rgp_hbm, rgp_ref),
     )
     extras = [pltpu.make_async_copy(a, b, table_sem.at[i]) for i, (a, b) in enumerate(pairs)]
     for copy in extras:
@@ -408,79 +426,100 @@
         slot(t)
         return carry
 
+    early_row = jnp.where(az % 2 == 0, rows - 1, 0)
+    late_row = rows - 1 - early_row
+
+    def outer(near):
+        for k in range(2):
+            @pl.when((az % 2 == 1 - k) == near)
+            def _():
+                fringe(k)
+
+    def row_of(s):
+        return jnp.where(s < rows - 2, s + 1, jnp.where(s == rows - 2, early_row, late_row))
+
     def shift(first, begin):
         def one(i, carry):
             @pl.when((i % PACE) == 0)
             def _():
                 slot(first + i // PACE)
 
-            s = begin + i // dates
-            p = jnp.where(s < rows - 2, s + 1, jnp.where(s == rows - 2, 0, rows - 1))
+            @pl.when((begin == 0) & (i == dates * (rows - 2)))
+            def _():
+                outer(True)
+
+            p = row_of(begin + i // dates)
             resample(p, i % dates, sizes, at_ref, ct_ref, pr_ref, wide, shifted, devs, stats)
             return carry
 
         return one
 
-    inner = dates * (rows - 2)
+    inner = dates * (rows - 1)
     lax.fori_loop(0, inner, shift(1, 0), 0)
-    lax.fori_loop(1 + -(-inner // PACE), HALO_SLOT, forward, 0)
-    for k in range(2):
-        fringe(k)
-    lax.fori_loop(0, 2 * dates, shift(HALO_SLOT, rows - 2), 0)
+    for copy in extras[3:]:
+        copy.wait()
+
+    paced = 1 + -(-inner // PACE)
+
+    def rest(s, carry):
+        @pl.when(paced + s < HALO_SLOT)
+        def _():
+            slot(paced + s)
+
+        settle(row_of(s), sizes, blk_ref, stats)
+        return carry
+
+    lax.fori_loop(0, rows - 1, rest, 0)
+    lax.fori_loop(paced + rows - 1, HALO_SLOT, forward, 0)
+    outer(False)
+    lax.fori_loop(0, dates, shift(max(HALO_SLOT, paced), rows - 1), 0)
+    settle(late_row, sizes, blk_ref, stats)
 
     @pl.when(mine == 0)
     def _():
         own.wait()
 
-    for copy in extras[3:]:
-        copy.wait()
-
-    begun = HALO_SLOT + -(-2 * dates // PACE)
+    begun = max(HALO_SLOT, paced) + -(-dates // PACE)
     last = pieces + max(0, count - 3) * LAG
 
-    def window_of(g):
-        return (g * (8 * LOOK_AZ) + 8 * LOOK_AZ - 1) // WIN
-
-    def due(g, after):
-        p = window_of(g)
-        ready = jnp.maximum((p + 1) * each + (count - 2) * LAG, begun + 1 + g + p + after)
-        return jnp.where(g < 0, begun, jnp.minimum(last, ready))
-
-    def group(g):
-        p = window_of(g)
-
-        lax.fori_loop(due(g - 1, 1), due(g, 0), forward, 0)
-
-        @pl.when((g == 0) | (p > window_of(g - 1)))
-        def _():
-            for c in range(2):
-                @pl.when(hops[c] == count - 1)
-                def _():
-                    for e in range(each):
-                        relay(c, p * each + e, False).wait_recv()
-
-            prepare(p, sizes, ref, ref32, devs, stats)
-            similarity(p, sizes, blk_ref, stats, sim_ref)
-
-        lax.fori_loop(due(g, 0), due(g, 1), forward, 0)
-        interferogram(g, sizes, rgp_ref, ref32, shifted, prod, pooled)
-
-    def patches(h, carry):
-        share = groups // halves
-
-        def one(i, inner):
-            group(h * share + i)
-            return inner
-
-        lax.fori_loop(0, share, one, 0)
-
-        @pl.when(h < halves - 1)
-        def _():
-            goldstein(h, dates, out_ref, dft_ref, blk_ref, pooled)
+    def due(j):
+        ready = jnp.maximum(j + 1 + (count - 2) * LAG, begun + (j + 1) // 2)
+        return jnp.where(j < 0, begun, jnp.minimum(last, ready))
+
+    def take(j):
+        lax.fori_loop(due(j - 1), due(j), forward, 0)
+        for c in range(2):
+            @pl.when(hops[c] == count - 1)
+            def _():
+                relay(c, j, False).wait_recv()
+
+        prepare(j // each, j % each, height, sizes, ref, ref32, devs, stats, root_stats)
+
+    def piece(j, carry):
+        take(j)
+
+        @pl.when(j % each == each - 1)
+        def _():
+            similarity(j // each, sizes, blk_ref, stats, root_stats, sim_ref)
+
+        g = (j + 1) * height // (8 * LOOK_AZ) - 1
+
+        @pl.when(g > j * height // (8 * LOOK_AZ) - 1)
+        def _():
+            interferogram(g, sizes, rgp_ref, ref32, shifted, pooled)
+
+        h = (j + 1) * height // (LOOK_AZ * PATCH) - 1
+
+        @pl.when(h > j * height // (LOOK_AZ * PATCH) - 1)
+        def _():
+            goldstein(h, dates, out_ref, left_ref, right_ref, blk_ref, pooled)
 
         return carry
 
-    lax.fori_loop(0, halves, patches, 0)
+    lax.fori_loop(0, pieces - 1, piece, 0)
+    take(pieces - 1)
+    similarity(rows - 1, sizes, blk_ref, stats, root_stats, sim_ref)
+    interferogram(groups - 1, sizes, rgp_ref, ref32, shifted, pooled)
 
     for c in range(2):
         @pl.when(hops[c] < count - 1)
@@ -503,11 +542,11 @@
             edge(k).wait_send()
 
 
-def finish(found_ref, early_ref, pooled_ref, dft_ref, blk_ref, sim_ref, out_ref):
+def finish(found_ref, early_ref, pooled_ref, left_ref, right_ref, blk_ref, sim_ref, out_ref):
     dates, _, early, _ = early_ref.shape
     sim_ref[...] = found_ref[...]
     out_ref[:, :, :early] = early_ref[...]
-    goldstein(early // PATCH, dates, out_ref, dft_ref, blk_ref, pooled_ref)
+    goldstein(early // PATCH, dates, out_ref, left_ref, right_ref, blk_ref, pooled_ref)
 
 
 def on_device(image, along, cross, present):
@@ -519,15 +558,15 @@
     looks = samples // LOOK_RG
     vmem = pl.BlockSpec(memory_space=pltpu.VMEM)
     dma = pltpu.SemaphoreType.DMA
-    dft, blocks, rg_pool = tables(samples)
+    left, right, blocks, rg_pool = tables(dates, samples)
     found, early, pooled = pl.pallas_call(
         kernel,
         out_shape=(
             jax.ShapeDtypeStruct((rows, dates, samples // WIN), F32),
             jax.ShapeDtypeStruct((dates, 2, (halves - 1) * PATCH, looks), F32),
-            jax.ShapeDtypeStruct((dates // 2, 2, 2, PATCH, looks), F32),
+            jax.ShapeDtypeStruct((dates, PATCH, 2 * looks), F32),
         ),
-        in_specs=[pl.BlockSpec(memory_space=pl.ANY)] * 7,
+        in_specs=[pl.BlockSpec(memory_space=pl.ANY)] * 8,
         out_specs=(vmem, vmem, vmem),
         scratch_shapes=[
             pltpu.VMEM((dates, 2, lines, samples), BF16),
@@ -537,17 +576,18 @@
             pltpu.VMEM((dates, 2, strips, lines, LANES), F32),
             pltpu.VMEM((dates, strips, lines, LANES), F32),
             pltpu.VMEM((2, strips, lines, LANES), F32),
-            pltpu.VMEM((2, dates, 16, samples), BF16),
-            pltpu.VMEM((rows, 3, strips, dates + 1, 8, LANES), F32),
+            pltpu.VMEM((rows, 3, strips, dates, 8, LANES), F32),
+            pltpu.VMEM((rows, 3, strips, 8, LANES), F32),
             pltpu.SMEM((rows, dates, samples // WIN), jnp.int32),
             pltpu.SMEM((rows, dates, samples // WIN), jnp.int32),
             pltpu.SMEM((dates, rows), jnp.int32),
-            pltpu.VMEM(dft.shape, F32),
+            pltpu.VMEM(left.shape, BF16),
+            pltpu.VMEM(right.shape, BF16),
             pltpu.VMEM(blocks.shape, BF16),
             pltpu.VMEM(rg_pool.shape, BF16),
             dma((2 * dates,)),
             dma(()),
-            dma((6,)),
+            dma((7,)),
             dma((2,)),
             dma((2,)),
             dma((2, pieces)),
@@ -558,7 +598,7 @@
             vmem_limit_bytes=62 * 1024 * 1024, collective_id=0, has_side_effects=True
         ),
     )(
-        along.transpose(1, 0, 2), cross.transpose(1, 0, 2), present, image, dft, blocks, rg_pool
+        along.transpose(1, 0, 2), cross.transpose(1, 0, 2), present, image, left, right, blocks, rg_pool
     )
     found, filtered = pl.pallas_call(
         finish,
@@ -566,9 +606,9 @@
             jax.ShapeDtypeStruct(found.shape, F32),
             jax.ShapeDtypeStruct((dates, 2, lines // LOOK_AZ, looks), F32),
         ),
-        in_specs=[vmem] * 5,
+        in_specs=[vmem] * 6,
         out_specs=(vmem, vmem),
-    )(found, early, pooled, dft, blocks)
+    )(found, early, pooled, left, right, blocks)
     return found.transpose(1, 0, 2), filtered
 
 

time: 35 us -> 32.7 us (0.934); the launches traced: 34.3 us -> 32.4 us
  Pallas kernels: 33.7 us -> 31.8 us
    pallas_call x1, Pallas kernels: 30.6 us -> 29 us  [on_device(): pl.pallas_call(kernel, out_shape=(jax.ShapeDtypeStruct((rows, dates, samp...]
where the time goes in v3:
time: 32.7 us; the launch traced here: 32.4 us
  Pallas kernels  31.8 us (97%)
  between operations  0.64 us (2%)
    pallas_call x1, Pallas kernels, on_device(): pl.pallas_call(kernel, out_shape=(jax.ShapeDtypeStruct((rows, dates, samp...  29 us
    pallas_call x1, Pallas kernels, on_device(): pl.pallas_call(finish, out_shape=(jax.ShapeDtypeStruct(found.shape, F32),...  2.75 us

profile of v3, /device:TPU:10, one launch (start us, length us, event | category | flops | bytes accessed | tf_op | source)
XLA Modules:
  0.0 32.4 jit_solution(14411467321957047061)
XLA Ops:
  0.6 29.0 %shard_map.95 = (f32[5,4,20]{2,1,0:T(4,128)}, f32[4,2,32,64]{3,2,1,0:T(8,128)}, f32[4,32,128]{2,1,0:T(8,128)}) custom-call(s32[5,4,20]{2,1,0:T(4,128)} %bitcast.3, s32[5,4,20]{2,1,0:T(4,128)} %bitcast.4, s32[4,5]{1,0:T(4,128)} %pr_hbm.1, bf16[4,2,320,1280]{3,2,1,0:T(8,128)(2,1)} %img_ref.1, bf16[2,128,256]{2,1,0:T(8,128)(2,1)} %constant.8.clone.left_hbm.left_ref, ...), custom_call_target="tpu_custom_call" | custom-call | tf_op jit(solution)/shard_map/pallas_call | solution.py:562
  29.7 2.7 %shard_map.96 = (f32[5,4,20]{2,1,0:T(4,128)}, f32[4,2,64,64]{3,2,1,0:T(8,128)}) custom-call(f32[5,4,20]{2,1,0:T(4,128)} %get-tuple-element.7.found_ref, f32[4,2,32,64]{3,2,1,0:T(8,128)} %get-tuple-element.8.early_ref, f32[4,32,128]{2,1,0:T(8,128)} %get-tuple-element.9.pooled_ref, bf16[2,128,256]{2,1,0:T(8,128)(2,1)} %constant.8.clone.left_hbm.left_ref, ...), custom_call_target="tpu_custom_call" | custom-call | tf_op jit(solution)/shard_map/pallas_call | solution.py:603

commit v4 on v3

--- a/solution.py
+++ b/solution.py
@@ -17,7 +17,12 @@
 LAG = 4
 PACE = 2
 HALO_SLOT = 12
-DUP = 3
+BEHIND = 4
+RATE = 2
+FILTER = 12
+MERGE = 2
+DUP_EVEN = 4
+DUP_ODD = 3
 
 VAR_EPS = 1e-05
 RMS_EPS = 1e-06
@@ -206,7 +211,7 @@
     sign = jnp.where(lax.broadcasted_iota(jnp.int32, (8, LANES), 1) < WIN, -1.0, 1.0)
     at = pl.ds(pl.multiple_of((g % (PATCH // 8)) * 8, 8), 8)
     for d in range(dates):
-        pooled[d, at, :] = sums[d, 0] + turned(sums[d, 1], sign)
+        pooled[g // (PATCH // 8), d, at, :] = sums[d, 0] + turned(sums[d, 1], sign)
 
 
 def goldstein(h, dates, out_ref, left_ref, right_ref, blk_ref, pooled):
@@ -249,8 +254,8 @@
 
 def kernel(
     at_hbm, ct_hbm, pr_hbm, img_ref, left_hbm, right_hbm, blk_hbm, rgp_hbm,
-    sim_ref, out_ref, pooled,
-    image, halo, ref, wide, shifted, devs, ref32, stats, root_stats,
+    sim_ref, out_ref, ending,
+    image, halo, ref, wide, shifted, devs, ref32, stats, root_stats, pooled,
     at_ref, ct_ref, pr_ref, left_ref, right_ref, blk_ref, rgp_ref,
     image_sem, root_sem, table_sem, halo_send, halo_recv, ref_send, ref_recv, dup_send,
 ):
@@ -320,10 +325,10 @@
             device_id_type=mesh_ids,
         )
 
-    dups = DUP if count > 2 else 0
+    dups = jnp.where(az % 2 == 0, DUP_EVEN, DUP_ODD) if count > 2 else 0
 
     def direct(c, e):
-        at = pl.ds(lines - (dups - e) * height, height)
+        at = pl.ds(pl.multiple_of(lines - (dups - e) * height, height), height)
         return pltpu.make_async_remote_copy(
             src_ref=img_ref.at[0, c, at],
             dst_ref=ref.at[c, at],
@@ -341,9 +346,13 @@
             return carry
 
         lax.fori_loop(0, pieces, launch, 0)
-        for e in range(dups):
+
+        def double(e, carry):
             for c in range(2):
                 direct(c, e).start()
+            return carry
+
+        lax.fori_loop(0, dups, double, 0)
 
     def sent(c):
         return jnp.where(hops[c] == count - 2, pieces - dups, jnp.where(hops[c] == count - 1, 0, pieces))
@@ -482,8 +491,10 @@
     begun = max(HALO_SLOT, paced) + -(-dates // PACE)
     last = pieces + max(0, count - 3) * LAG
 
+    behind = max((count - 2) * BEHIND, (count - 3) * LAG)
+
     def due(j):
-        ready = jnp.maximum(j + 1 + (count - 2) * LAG, begun + (j + 1) // 2)
+        ready = jnp.maximum(j + 1 + behind, begun + (j + 1) // RATE)
         return jnp.where(j < 0, begun, jnp.minimum(last, ready))
 
     def take(j):
@@ -498,9 +509,9 @@
     def piece(j, carry):
         take(j)
 
-        @pl.when(j % each == each - 1)
-        def _():
-            similarity(j // each, sizes, blk_ref, stats, root_stats, sim_ref)
+        @pl.when((j >= each) & (j % each == MERGE))
+        def _():
+            similarity(j // each - 1, sizes, blk_ref, stats, root_stats, sim_ref)
 
         g = (j + 1) * height // (8 * LOOK_AZ) - 1
 
@@ -508,11 +519,10 @@
         def _():
             interferogram(g, sizes, rgp_ref, ref32, shifted, pooled)
 
-        h = (j + 1) * height // (LOOK_AZ * PATCH) - 1
-
-        @pl.when(h > j * height // (LOOK_AZ * PATCH) - 1)
-        def _():
-            goldstein(h, dates, out_ref, left_ref, right_ref, blk_ref, pooled)
+        for h in range(halves - 1):
+            @pl.when(j == min(pieces - 2, h * (pieces // halves) + FILTER))
+            def _():
+                goldstein(h, dates, out_ref, left_ref, right_ref, blk_ref, pooled.at[h])
 
         return carry
 
@@ -520,6 +530,7 @@
     take(pieces - 1)
     similarity(rows - 1, sizes, blk_ref, stats, root_stats, sim_ref)
     interferogram(groups - 1, sizes, rgp_ref, ref32, shifted, pooled)
+    ending[...] = pooled[halves - 1]
 
     for c in range(2):
         @pl.when(hops[c] < count - 1)
@@ -532,9 +543,12 @@
 
     @pl.when(mine == 0)
     def _():
-        for e in range(dups):
+        def doubled(e, carry):
             for c in range(2):
                 direct(c, e).wait_send()
+            return carry
+
+        lax.fori_loop(0, dups, doubled, 0)
 
     for k in range(2):
         @pl.when(sends[k])
@@ -578,6 +592,7 @@
             pltpu.VMEM((2, strips, lines, LANES), F32),
             pltpu.VMEM((rows, 3, strips, dates, 8, LANES), F32),
             pltpu.VMEM((rows, 3, strips, 8, LANES), F32),
+            pltpu.VMEM((halves, dates, PATCH, 2 * looks), F32),
             pltpu.SMEM((rows, dates, samples // WIN), jnp.int32),
             pltpu.SMEM((rows, dates, samples // WIN), jnp.int32),
             pltpu.SMEM((dates, rows), jnp.int32),
@@ -592,7 +607,7 @@
             dma((2,)),
             dma((2, pieces)),
             dma((2, pieces)),
-            dma((2, DUP)),
+            dma((2, max(DUP_EVEN, DUP_ODD))),
         ],
         compiler_params=pltpu.CompilerParams(
             vmem_limit_bytes=62 * 1024 * 1024, collective_id=0, has_side_effects=True

time: 32.7 us -> 32.3 us (0.988)
  Pallas kernels: 31.8 us -> 31.4 us
    pallas_call x1, Pallas kernels: 29 us -> 28.6 us  [on_device(): pl.pallas_call(kernel, out_shape=(jax.ShapeDtypeStruct((rows, dates, samp...]
where the time goes in v4:
time: 32.3 us; the launch traced here: 32 us
  Pallas kernels  31.4 us (97%)
  between operations  0.64 us (2%)
    pallas_call x1, Pallas kernels, on_device(): pl.pallas_call(kernel, out_shape=(jax.ShapeDtypeStruct((rows, dates, samp...  28.6 us
    pallas_call x1, Pallas kernels, on_device(): pl.pallas_call(finish, out_shape=(jax.ShapeDtypeStruct(found.shape, F32),...  2.75 us

profile of v4, /device:TPU:10, one launch (start us, length us, event | category | flops | bytes accessed | tf_op | source)
XLA Modules:
  0.0 32.0 jit_solution(17859034866168178721)
XLA Ops:
  0.6 28.6 %shard_map.95 = (f32[5,4,20]{2,1,0:T(4,128)}, f32[4,2,32,64]{3,2,1,0:T(8,128)}, f32[4,32,128]{2,1,0:T(8,128)}) custom-call(s32[5,4,20]{2,1,0:T(4,128)} %bitcast.3, s32[5,4,20]{2,1,0:T(4,128)} %bitcast.4, s32[4,5]{1,0:T(4,128)} %pr_hbm.1, bf16[4,2,320,1280]{3,2,1,0:T(8,128)(2,1)} %img_ref.1, bf16[2,128,256]{2,1,0:T(8,128)(2,1)} %constant.8.clone.left_hbm.left_ref, ...), custom_call_target="tpu_custom_call" | custom-call | tf_op jit(solution)/shard_map/pallas_call | solution.py:576
  29.3 2.7 %shard_map.96 = (f32[5,4,20]{2,1,0:T(4,128)}, f32[4,2,64,64]{3,2,1,0:T(8,128)}) custom-call(f32[5,4,20]{2,1,0:T(4,128)} %get-tuple-element.7.found_ref, f32[4,2,32,64]{3,2,1,0:T(8,128)} %get-tuple-element.8.early_ref, f32[4,32,128]{2,1,0:T(8,128)} %get-tuple-element.9.pooled_ref, bf16[2,128,256]{2,1,0:T(8,128)(2,1)} %constant.8.clone.left_hbm.left_ref, ...), custom_call_target="tpu_custom_call" | custom-call | tf_op jit(solution)/shard_map/pallas_call | solution.py:618

commit v5 on v4

--- a/solution.py
+++ b/solution.py
@@ -14,7 +14,7 @@
 PATCH = 32
 LANES = 128
 PIECE = 16
-LAG = 4
+LAG = 5
 PACE = 2
 HALO_SLOT = 12
 BEHIND = 4
@@ -284,6 +284,18 @@
         c = i % 2
         return pltpu.make_async_copy(img_ref.at[d, c], image.at[d, c], image_sem.at[i])
 
+    barrier = pltpu.get_barrier_semaphore()
+    for target in targets:
+        pl.semaphore_signal(barrier, inc=1, device_id={"date": target}, device_id_type=mesh_ids)
+
+    @pl.when(az > 0)
+    def _():
+        pl.semaphore_signal(barrier, inc=1, device_id={"az": az - 1}, device_id_type=mesh_ids)
+
+    @pl.when(az < az_count - 1)
+    def _():
+        pl.semaphore_signal(barrier, inc=1, device_id={"az": az + 1}, device_id_type=mesh_ids)
+
     for i in range(2 * dates):
         load(i).start()
     pairs = (
@@ -298,18 +310,6 @@
     @pl.when(mine == 0)
     def _():
         own.start()
-
-    barrier = pltpu.get_barrier_semaphore()
-    for target in targets:
-        pl.semaphore_signal(barrier, inc=1, device_id={"date": target}, device_id_type=mesh_ids)
-
-    @pl.when(az > 0)
-    def _():
-        pl.semaphore_signal(barrier, inc=1, device_id={"az": az - 1}, device_id_type=mesh_ids)
-
-    @pl.when(az < az_count - 1)
-    def _():
-        pl.semaphore_signal(barrier, inc=1, device_id={"az": az + 1}, device_id_type=mesh_ids)
 
     peers = 2 + jnp.where(az > 0, 1, 0) + jnp.where(az < az_count - 1, 1, 0)
     pl.semaphore_wait(barrier, peers)

time: 32.3 us -> 32.2 us (level)
  no operation moved by 1% of the time
where the time goes in v5:
time: 32.2 us; the launch traced here: 32 us
  Pallas kernels  31.4 us (98%)
  between operations  0.64 us (2%)
    pallas_call x1, Pallas kernels, on_device(): pl.pallas_call(kernel, out_shape=(jax.ShapeDtypeStruct((rows, dates, samp...  28.6 us
    pallas_call x1, Pallas kernels, on_device(): pl.pallas_call(finish, out_shape=(jax.ShapeDtypeStruct(found.shape, F32),...  2.75 us

profile of v5, /device:TPU:10, one launch (start us, length us, event | category | flops | bytes accessed | tf_op | source)
XLA Modules:
  0.0 32.0 jit_solution(10899532103109495975)
XLA Ops:
  0.6 28.6 %shard_map.95 = (f32[5,4,20]{2,1,0:T(4,128)}, f32[4,2,32,64]{3,2,1,0:T(8,128)}, f32[4,32,128]{2,1,0:T(8,128)}) custom-call(s32[5,4,20]{2,1,0:T(4,128)} %bitcast.3, s32[5,4,20]{2,1,0:T(4,128)} %bitcast.4, s32[4,5]{1,0:T(4,128)} %pr_hbm.1, bf16[4,2,320,1280]{3,2,1,0:T(8,128)(2,1)} %img_ref.1, bf16[2,128,256]{2,1,0:T(8,128)(2,1)} %constant.8.clone.left_hbm.left_ref, ...), custom_call_target="tpu_custom_call" | custom-call | tf_op jit(solution)/shard_map/pallas_call | solution.py:576
  29.3 2.7 %shard_map.96 = (f32[5,4,20]{2,1,0:T(4,128)}, f32[4,2,64,64]{3,2,1,0:T(8,128)}) custom-call(f32[5,4,20]{2,1,0:T(4,128)} %get-tuple-element.7.found_ref, f32[4,2,32,64]{3,2,1,0:T(8,128)} %get-tuple-element.8.early_ref, f32[4,32,128]{2,1,0:T(8,128)} %get-tuple-element.9.pooled_ref, bf16[2,128,256]{2,1,0:T(8,128)(2,1)} %constant.8.clone.left_hbm.left_ref, ...), custom_call_target="tpu_custom_call" | custom-call | tf_op jit(solution)/shard_map/pallas_call | solution.py:618
